TPU v7x, 32 devices: a whole 2x2x4 slice. The times are simulated.
32 devices in a mesh: dom: 8 (over z, y), rep: 4 (over x, core).
Axes of the slice: x: 2, y: 2, z: 4, core: 2. Of those that a mesh axis runs over, the one named last changes fastest.
Arguments:
- features: float32 [4, 2, 2048, 128], P('rep', None, 'dom'), may hold values from -6 to 6
- edge_src: int32 [4, 2, 2048, 10], P('rep', None, 'dom'), may hold values from 0 to 319, as said below
- node_degree: int32 [4, 2, 2048], P('rep', None, 'dom'), may hold values from 1 to 10, as said below
- send_rows: int32 [4, 2, 64, 8], P('rep', None, 'dom'), may hold values from 0 to 255
- pair_src: int32 [4, 2, 4096], P('rep', None, 'dom'), may hold values from 0 to 255
- pair_dst: int32 [4, 2, 4096], P('rep', None, 'dom'), may hold values from 0 to 319
- pair_live: int32 [4, 2, 8], P('rep', None, 'dom'), may hold values from 1 to 256, as said below
- proj_one: float32 [128, 768], replicated, may hold values from -0.5 to 0.5
- proj_two: float32 [256, 576], replicated, may hold values from -0.375 to 0.375
- head_weight: float32 [64, 64], replicated, may hold values from -0.5 to 0.5
- vectors: float32 [5, 256], replicated, may hold values from -1.5 to 1.5
- biases: float32 [2, 64], replicated, may hold values from -1.5 to 1.5
- first_one: float32 [128, 768], replicated, may hold values from -0.0078125 to 0.0078125
- first_two: float32 [256, 576], replicated, may hold values from -0.0078125 to 0.0078125
- first_head: float32 [64, 64], replicated, may hold values from -0.0078125 to 0.0078125
- first_vectors: float32 [5, 256], replicated, may hold values from -0.0234375 to 0.0234375
- first_biases: float32 [2, 64], replicated, may hold values from -0.0234375 to 0.0234375
- second_one: float32 [128, 768], replicated, may hold values from 1.525879e-08 to 1.2207032e-07
- second_two: float32 [256, 576], replicated, may hold values from 1.525879e-08 to 1.2207032e-07
- second_head: float32 [64, 64], replicated, may hold values from 1.525879e-08 to 1.2207032e-07
- second_vectors: float32 [5, 256], replicated, may hold values from 1.373291e-07 to 1.0986328e-06
- second_biases: float32 [2, 64], replicated, may hold values from 1.373291e-07 to 1.0986328e-06
Outputs:
- loss_sum: float32 [], replicated
- pair_count: float32 [], replicated
- next_first_one: float32 [128, 768], replicated
- next_second_one: float32 [128, 768], replicated
- next_proj_one: float32 [128, 768], replicated
- next_first_two: float32 [256, 576], replicated
- next_second_two: float32 [256, 576], replicated
- next_proj_two: float32 [256, 576], replicated
- next_first_head: float32 [64, 64], replicated
- next_second_head: float32 [64, 64], replicated
- next_head_weight: float32 [64, 64], replicated
- next_first_vectors: float32 [5, 256], replicated
- next_second_vectors: float32 [5, 256], replicated
- next_vectors: float32 [5, 256], replicated
- next_first_biases: float32 [2, 64], replicated
- next_second_biases: float32 [2, 64], replicated
- next_biases: float32 [2, 64], replicated
Inputs may be any that keep to these rules, and one draw needn't show every extreme that they name: `node_degree`: every node has at least one live edge slot; every eighth node of a partition has all 10. `edge_src`: indices below 256 name own rows; the others name received rows. `pair_live`: the last partition has all its slots live.
All inputs are finite; a program needn't handle non-finite values.
Results may differ from a plain program's by a relative error of at most 0.0063.
Values may be sent and summed in bfloat16 or wider, within the bound.
A program may use at most 192 MiB of HBM per device.

v0:
```python
import jax
import jax.numpy as jnp
from jax import lax
from jax.sharding import PartitionSpec as P

HID = 256
HEADS = 4
HEAD = 64
FAN = 10
PAIRS = 512
MB = 2
STEP = 5


eps_norm = 1e-05
beta_one = 0.9
beta_two = 0.999
rate_step = 0.05
decay_rate = 0.01
eps_adam = 1e-08


def attend(gathered, target, resid, vecs, degree):
    rows = gathered.shape[0]
    mixed = jax.nn.silu(gathered + target[:, None, :])
    score = jnp.sum((mixed * vecs[0]).reshape(rows, FAN, HEADS, -1), axis=-1)
    live = (jnp.arange(FAN)[None, :] < degree[:, None])[:, :, None]
    score = jnp.where(live, score, -1e30)
    top = jnp.max(score, axis=1, keepdims=True)
    weight = jnp.where(live, jnp.exp(score - top), 0.0)
    alpha = weight / jnp.sum(weight, axis=1, keepdims=True)
    message = jnp.sum(alpha[..., None] * gathered.reshape(rows, FAN, HEADS, -1), axis=1)
    if len(vecs) == 4:
        summed = message.reshape(rows, -1) + vecs[1] + resid
        centred = summed - jnp.mean(summed, axis=-1, keepdims=True)
        spread = jnp.mean(centred * centred, axis=-1, keepdims=True)
        normed = centred * lax.rsqrt(spread + eps_norm) * vecs[2] + vecs[3]
        return jax.nn.elu(normed)
    return jnp.mean(message, axis=1) + vecs[1] + resid


def transposed(left, right):
    return lax.dot_general(
        left, right, (((0,), (0,)), ((), ())), preferred_element_type=jnp.float32
    )


def layer_forward(hidden, weight, vecs, edges, degree, sends):
    hid_low = hidden.astype(jnp.bfloat16)
    weight_low = weight.astype(jnp.bfloat16)
    proj = jnp.dot(hid_low, weight_low, preferred_element_type=jnp.float32)
    source = proj[:, :HID].astype(jnp.bfloat16)
    halo_in = None
    outgoing = source[sends.reshape(-1)].reshape(sends.shape[0], sends.shape[1], HID)
    incoming = lax.all_to_all(outgoing, "dom", split_axis=0, concat_axis=0, tiled=True).reshape(
        -1, HID
    )
    table = jnp.concatenate([source, incoming], axis=0)
    target = proj[:, HID : 2 * HID]
    resid = proj[:, 2 * HID :]
    result = attend(table[edges].astype(jnp.float32), target, resid, vecs, degree)
    return (result, (hid_low, weight_low, table, target, resid, halo_in))


def layer_backward(grad_out, kept, vecs, edges, degree, sends, first_layer):
    hid_low, weight_low, table, target, resid, halo_in = kept
    rows = target.shape[0]

    def piece(gathered, tgt, res, values):
        return attend(gathered, tgt, res, values, degree)

    _, pullback = jax.vjp(piece, table[edges].astype(jnp.float32), target, resid, vecs)
    d_gath, d_target, d_resid, d_vecs = pullback(grad_out)
    d_table = jnp.zeros(table.shape, jnp.float32).at[edges.reshape(-1)].add(d_gath.reshape(-1, HID))
    if first_layer:
        d_own = jnp.concatenate([d_table[:rows], d_target, d_resid], axis=1).astype(jnp.bfloat16)
        d_weight = transposed(hid_low, d_own)
        tail_low = d_table[rows:].astype(jnp.bfloat16)
        returned = lax.all_to_all(
            tail_low.reshape(sends.shape[0], sends.shape[1], HID),
            "dom",
            split_axis=0,
            concat_axis=0,
            tiled=True,
        )
        halo_part = transposed(hid_low[sends.reshape(-1)], returned.reshape(-1, HID))
        d_weight = d_weight.at[:, :HID].add(halo_part)
        return (None, d_weight, d_vecs)
    returned = lax.all_to_all(
        d_table[rows:].reshape(sends.shape[0], sends.shape[1], HID).astype(jnp.bfloat16),
        "dom",
        split_axis=0,
        concat_axis=0,
        tiled=True,
    ).astype(jnp.float32)
    d_source = d_table[:rows].at[sends.reshape(-1)].add(returned.reshape(-1, HID))
    d_proj = jnp.concatenate([d_source, d_target, d_resid], axis=1).astype(jnp.bfloat16)
    d_weight = transposed(hid_low, d_proj)
    d_input = lax.dot_general(
        d_proj, weight_low, (((1,), (1,)), ((), ())), preferred_element_type=jnp.float32
    )
    return (d_input, d_weight, d_vecs)


def micro_step(params, feats, edges, degree, sends, pair_src, pair_dst, live_count):
    proj_one, proj_two, head_weight, vectors, biases = params
    vecs_one = (vectors[0], vectors[1], vectors[2], vectors[3])
    vecs_two = (vectors[4], biases[0])
    first_out, kept_one = layer_forward(feats, proj_one, vecs_one, edges, degree, sends)
    second_out, kept_two = layer_forward(first_out, proj_two, vecs_two, edges, degree, sends)
    second_low = second_out.astype(jnp.bfloat16)
    head_low = head_weight.astype(jnp.bfloat16)
    embed = jnp.dot(second_low, head_low, preferred_element_type=jnp.float32) + biases[1]
    rows = embed.shape[0]
    outgoing = embed[sends.reshape(-1)].reshape(sends.shape[0], sends.shape[1], HEAD)
    incoming = lax.all_to_all(outgoing, "dom", split_axis=0, concat_axis=0, tiled=True)
    table = jnp.concatenate([embed, incoming.reshape(-1, HEAD)], axis=0)
    first = embed[pair_src]
    second = table[pair_dst]
    score = jnp.sum(first * second, axis=-1)
    slot = jnp.arange(pair_src.shape[0], dtype=jnp.int32)
    positive = slot < PAIRS // 2
    live = slot % (PAIRS // 2) < live_count
    terms = jnp.where(positive, jax.nn.softplus(-score), jax.nn.softplus(score))
    loss = jnp.sum(jnp.where(live, terms, 0.0))
    d_score = jnp.where(
        live, jnp.where(positive, -jax.nn.sigmoid(-score), jax.nn.sigmoid(score)), 0.0
    )
    d_table = jnp.zeros(table.shape, jnp.float32).at[pair_dst].add(d_score[:, None] * first)
    returned = lax.all_to_all(
        d_table[rows:].reshape(sends.shape[0], sends.shape[1], HEAD).astype(jnp.bfloat16),
        "dom",
        split_axis=0,
        concat_axis=0,
        tiled=True,
    ).astype(jnp.float32)
    d_embed = d_table[:rows].at[pair_src].add(d_score[:, None] * second)
    d_embed = d_embed.at[sends.reshape(-1)].add(returned.reshape(-1, HEAD))
    d_embed_low = d_embed.astype(jnp.bfloat16)
    d_head = transposed(second_low, d_embed_low)
    d_second = lax.dot_general(
        d_embed_low, head_low, (((1,), (1,)), ((), ())), preferred_element_type=jnp.float32
    )
    d_first, d_proj_two, d_vecs_two = layer_backward(
        d_second, kept_two, vecs_two, edges, degree, sends, False
    )
    _, d_proj_one, d_vecs_one = layer_backward(
        d_first, kept_one, vecs_one, edges, degree, sends, True
    )
    d_vectors = jnp.stack(
        [d_vecs_one[0], d_vecs_one[1], d_vecs_one[2], d_vecs_one[3], d_vecs_two[0]]
    )
    d_biases = jnp.stack([d_vecs_two[1], jnp.sum(d_embed, axis=0)])
    return (loss, (d_proj_one, d_proj_two, d_head, d_vectors, d_biases))


def adamw(param, grad, first, second):
    first = beta_one * first + (1.0 - beta_one) * grad
    second = beta_two * second + (1.0 - beta_two) * grad * grad
    fhat = first / (1.0 - beta_one**STEP)
    shat = second / (1.0 - beta_two**STEP)
    return (
        first,
        second,
        param - rate_step * (fhat / (jnp.sqrt(shat) + eps_adam) + decay_rate * param),
    )


def body(
    features,
    edge_src,
    node_degree,
    send_rows,
    pair_src,
    pair_dst,
    pair_live,
    proj_one,
    proj_two,
    head_weight,
    vectors,
    biases,
    first_one,
    first_two,
    first_head,
    first_vectors,
    first_biases,
    second_one,
    second_two,
    second_head,
    second_vectors,
    second_biases,
):
    params = (proj_one, proj_two, head_weight, vectors, biases)
    firsts = (first_one, first_two, first_head, first_vectors, first_biases)
    seconds = (second_one, second_two, second_head, second_vectors, second_biases)
    grads = tuple((jnp.zeros_like(p) for p in params))
    loss_local = jnp.zeros((), jnp.float32)
    for batch in range(MB):
        loss, more = micro_step(
            params,
            features[0, batch],
            edge_src[0, batch],
            node_degree[0, batch],
            send_rows[0, batch],
            pair_src[0, batch],
            pair_dst[0, batch],
            pair_live[0, batch, 0],
        )
        loss_local = loss_local + loss
        grads = tuple((g + m for g, m in zip(grads, more)))
    count_local = 2.0 * jnp.sum(pair_live).astype(jnp.float32)
    outs = []
    summed = lax.psum(
        (grads[0], grads[1], grads[2], grads[3], grads[4], loss_local, count_local), ("dom", "rep")
    )
    loss_sum = summed[5]
    pair_count = summed[6]
    for index in range(5):
        outs.extend(adamw(params[index], summed[index] / pair_count, firsts[index], seconds[index]))
    return (
        loss_sum,
        pair_count,
        outs[0],
        outs[1],
        outs[2],
        outs[3],
        outs[4],
        outs[5],
        outs[6],
        outs[7],
        outs[8],
        outs[9],
        outs[10],
        outs[11],
        outs[12],
        outs[13],
        outs[14],
    )


def solution(mesh):
    placed = (
        P("rep", None, "dom", None),
        P("rep", None, "dom", None),
        P("rep", None, "dom"),
        P("rep", None, "dom", None),
        P("rep", None, "dom"),
        P("rep", None, "dom"),
        P("rep", None, "dom"),
        P(),
        P(),
        P(),
        P(),
        P(),
        P(),
        P(),
        P(),
        P(),
        P(),
        P(),
        P(),
        P(),
        P(),
        P(),
    )
    return jax.shard_map(
        body,
        mesh=mesh,
        in_specs=placed,
        out_specs=(
            P(),
            P(),
            P(),
            P(),
            P(),
            P(),
            P(),
            P(),
            P(),
            P(),
            P(),
            P(),
            P(),
            P(),
            P(),
            P(),
            P(),
        ),
        check_vma=False,
    )
```

profile of v0, /device:TPU:0, one launch (start us, length us, event | category | flops | bytes accessed | tf_op | source)
XLA Modules:
  0.0 859.4 jit_solution(7064971588253980328)
XLA Ops:
  11.8 7.3 all-to-all-start.3
  45.5 7.6 gather_fusion.8
  57.0 7.6 gather_fusion.1
  69.4 11.8 %multiply_reduce_fusion.7 = (f32[256,10,4]{2,1,0:T(8,128)S(1)}, f32[256,10,4]{2,1,0:T(8,128)}) fusion(f32[256,10,4,64]{3,2,1,0:T(4,128)} %reshape.1126, f32[256,4,64]{2,1,0:T(4,128)} %copy.380, f32[4,64]{1,0:T(4,128)S(1)} %mul.923, f32[256,10,4,64]{3,2,1,0:T(4,128)} %reshape.1124, f32[256,4,64]{2,1,0:T(4,128)} %copy.366), kind=kLoop, calls=%fused_computation.43 | loop fusion | flops 9154560 | bytes 5850112 | tf_op jit(solution)/shard_map/reduce_sum | solution.py:26
  102.3 8.2 multiply_reduce_fusion.10
  141.2 6.5 mul.926
  153.4 6.5 mul.943
  172.2 8.1 gather_fusion.10
  186.0 8.1 gather_fusion.3
  199.4 10.2 %multiply_reduce_fusion.5 = (f32[256,10,4]{2,1,0:T(8,128)S(1)}, f32[256,10,4]{2,1,0:T(8,128)S(1)}) fusion(f32[256,10,4,64]{3,2,1,0:T(4,128)} %reshape.1127, f32[256,4,64]{2,1,0:T(4,128)} %copy.386, f32[4,64]{1,0:T(4,128)S(1)} %mul.935, f32[256,10,4,64]{3,2,1,0:T(4,128)} %reshape.1125, f32[256,4,64]{2,1,0:T(4,128)} %copy.372), kind=kLoop, calls=%fused_computation.41 | loop fusion | flops 9154560 | bytes 5850112 | tf_op jit(solution)/shard_map/reduce_sum | solution.py:26
  227.4 6.6 multiply_reduce_fusion.8
  255.6 6.5 mul.938
  267.9 6.5 mul.951
  387.6 11.8 %multiply_reduce_fusion.12 = (f32[256]{0:T(256)}, bf16[256,256]{1,0:T(8,128)(2,1)}, f32[256,10,256]{2,1,0:T(8,128)}, bf16[256,256]{1,0:T(8,128)(2,1)}, f32[256]{0:T(256)}, /*index=5*/f32[256,10,256]{2,1,0:T(8,128)}) fusion(f32[256,10,256]{2,1,0:T(8,128)} %copy.415, f32[256]{0:T(256)S(1)} %bitcast.206, f32[256,10,256]{2,1,0:T(8,128)} %reshape.1367, ...), kind=kLoop, calls=%fused_computation.60 | loop fusion | flops 19529216 | bytes 16518144 | tf_op jit(solution)/shard_map/transpose(jvp())/reduce_sum | solution.py:26
  403.9 6.5 broadcast_in_dim.305.clone
  423.3 15.1 %scatter_custom_fusion.3 = f32[320,256]{1,0:T(8,128)S(1)} fusion(s32[2560]{0:T(1024)} %fusion.159, f32[2560,256]{1,0:T(8,128)} %add.696, f32[2560,256]{1,0:T(8,128)} %reshape.1100, f32[2560,256]{1,0:T(8,128)} %mul.957, f32[2560,256]{1,0:T(8,128)} %broadcast_in_dim.301, f32[]{:T(128)} %constant.207.clone.1, f32[256]{0:T(256)S(1)} %bitcast.207, ...), kind=kCustom, calls=%fused_computation.75 | custom fusion | flops 8519680 | bytes 10815488 | tf_op jit(solution)/shard_map/scatter-add | solution.py:74
  447.3 6.5 broadcast_in_dim.323.clone
  466.7 15.8 %scatter_custom_fusion.9 = f32[320,256]{1,0:T(8,128)} fusion(s32[2560]{0:T(1024)} %fusion.160, f32[2560,256]{1,0:T(8,128)} %add.710, f32[2560,256]{1,0:T(8,128)} %reshape.1109, f32[2560,256]{1,0:T(8,128)} %mul.1011, f32[2560,256]{1,0:T(8,128)} %broadcast_in_dim.319, f32[]{:T(128)} %constant.207.clone.1, f32[256]{0:T(256)S(1)} %bitcast.208, ...), kind=kCustom, calls=%fused_computation.83 | custom fusion | flops 8519680 | bytes 10815488 | tf_op jit(solution)/shard_map/scatter-add | solution.py:74
  560.0 11.6 %multiply_reduce_fusion.13 = (f32[256]{0:T(256)}, bf16[256,256]{1,0:T(8,128)(2,1)}, f32[256,10,256]{2,1,0:T(8,128)}, bf16[256,256]{1,0:T(8,128)(2,1)}, f32[256]{0:T(256)}, /*index=5*/f32[256,10,256]{2,1,0:T(8,128)}) fusion(f32[256,10,256]{2,1,0:T(8,128)} %copy.423, f32[256]{0:T(256)S(1)} %bitcast.204, f32[256,10,256]{2,1,0:T(8,128)} %reshape.1366, ...), kind=kLoop, calls=%fused_computation.61 | loop fusion | flops 19529216 | bytes 16518144 | tf_op jit(solution)/shard_map/transpose(jvp())/reduce_sum | solution.py:26
  576.1 6.6 broadcast_in_dim.314.clone
  595.4 15.2 %scatter_custom_fusion.5 = f32[320,256]{1,0:T(8,128)S(1)} fusion(s32[2560]{0:T(1024)} %fusion.159, f32[2560,256]{1,0:T(8,128)} %add.701, f32[2560,256]{1,0:T(8,128)} %reshape.1104, f32[2560,256]{1,0:T(8,128)} %mul.956, f32[2560,256]{1,0:T(8,128)} %broadcast_in_dim.310, f32[256]{0:T(256)S(1)} %bitcast.205, f32[]{:T(128)} %constant.207.clone.1, ...), kind=kCustom, calls=%fused_computation.79 | custom fusion | flops 8519680 | bytes 10815488 | tf_op jit(solution)/shard_map/scatter-add | solution.py:74
  638.9 15.4 %scatter_custom_fusion.11 = f32[320,256]{1,0:T(8,128)S(1)} fusion(s32[2560]{0:T(1024)} %fusion.160, f32[2560,256]{1,0:T(8,128)S(1)} %copy-done.13, f32[2560,256]{1,0:T(8,128)} %reshape.1113, f32[2560,256]{1,0:T(8,128)} %mul.1010, f32[2560,256]{1,0:T(8,128)} %broadcast_in_dim.328, f32[256]{0:T(256)} %bitcast.203, f32[]{:T(128)} %constant.207.clone.1, ...), kind=kCustom, calls=%fused_computation.87 | custom fusion | flops 8519680 | bytes 10815488 | tf_op jit(solution)/shard_map/scatter-add | solution.py:74
  660.8 41.4 %all-reduce = (f32[]{:T(128)}, f32[]{:T(128)}, f32[64,64]{1,0:T(8,128)S(1)}, f32[5,256]{1,0:T(8,128)S(1)}, f32[2,64]{1,0:T(2,128)S(1)}) all-reduce(f32[]{:T(128)S(6)} %add.690, f32[]{:T(128)S(6)} %mul_shard_map.3, f32[64,64]{1,0:T(8,128)S(1)} %copy-done.83, f32[5,256]{1,0:T(8,128)S(1)} %add.737, ...), channel_id=1, replica_groups=mesh['dom'=8,'rep'=4] {'dom','rep'}, use_global_device_ids=true, to_apply=%region_24.25 | all-reduce | flops 5506 | bytes 44048 | tf_op jit(solution)/shard_map/psum | solution.py:213
  719.8 124.4 %all-reduce.4.cloned.1.call-done = (f32[128,768]{0,1:T(8,128)}, f32[256,576]{0,1:T(8,128)}) async-done(((f32[128,768]{0,1:T(8,128)}, f32[256,576]{0,1:T(8,128)}), (f32[128,768]{0,1:T(8,128)}, f32[256,576]{0,1:T(8,128)})) %all-reduce.4.cloned.1.call-update) | async-done | bytes 983056 | tf_op jit(solution)/shard_map/psum | solution.py:213
  (583 shorter events, 469.3 us)
Async XLA Ops:
  10.5 105.7 %copy-start.106 = (s32[1024]{0:T(1024)}, s32[1024]{0:T(1024)S(1)}, u32[]{:S(2)}) copy-start(s32[1024]{0:T(1024)S(1)} %pad_clamp_fusion.4) | copy-start | bytes 12292
  11.8 27.4 %all-to-all-start.3 = ((bf16[8,8,256]{2,1,0:T(8,128)(2,1)}), bf16[8,8,256]{2,1,0:T(8,128)(2,1)S(1)}, u32[]{:S(2)}, u32[]{:S(2)}) async-start(bf16[8,8,256]{2,1,0:T(8,128)(2,1)} %bitcast.27), calls=%async_computation.3 | async-start | bytes 65536 | tf_op jit(solution)/shard_map/all_to_all | solution.py:55
  24.8 99.8 %copy-start.94 = (f32[1,256]{1,0:T(1,128)}, f32[1,256]{1,0:T(1,128)S(1)}, u32[]{:S(2)}) copy-start(f32[1,256]{1,0:T(1,128)S(1)} %get-tuple-element.240) | copy-start | bytes 3076
  25.0 113.0 %copy-start.107 = (s32[1024]{0:T(1024)}, s32[1024]{0:T(1024)S(1)}, u32[]{:S(2)}) copy-start(s32[1024]{0:T(1024)S(1)} %pad_clamp_fusion.7) | copy-start | bytes 12292
  39.2 17.8 %all-to-all-start = ((bf16[8,8,256]{2,1,0:T(8,128)(2,1)}), bf16[8,8,256]{2,1,0:T(8,128)(2,1)S(1)}, u32[]{:S(2)}, u32[]{:S(2)}) async-start(bf16[8,8,256]{2,1,0:T(8,128)(2,1)} %bitcast.4), calls=%async_computation | async-start | bytes 65536 | tf_op jit(solution)/shard_map/all_to_all | solution.py:55
  113.9 393.9 %copy-start.18 = (f32[256,256]{1,0:T(8,128)}, f32[256,256]{1,0:T(8,128)S(1)}, u32[]{:S(2)}) copy-start(f32[256,256]{1,0:T(8,128)S(1)} %get-tuple-element.268) | copy-start | bytes 786436
  118.4 47.3 %all-to-all-start.4 = ((bf16[8,8,256]{2,1,0:T(8,128)(2,1)}), bf16[8,8,256]{2,1,0:T(8,128)(2,1)S(1)}, u32[]{:S(2)}, u32[]{:S(2)}) async-start(bf16[8,8,256]{2,1,0:T(8,128)(2,1)} %bitcast.32), calls=%async_computation.4 | async-start | bytes 65536 | tf_op jit(solution)/shard_map/all_to_all | solution.py:55
  165.7 20.0 %all-to-all-start.1 = ((bf16[8,8,256]{2,1,0:T(8,128)(2,1)}), bf16[8,8,256]{2,1,0:T(8,128)(2,1)S(1)}, u32[]{:S(2)}, u32[]{:S(2)}) async-start(bf16[8,8,256]{2,1,0:T(8,128)(2,1)} %bitcast.12), calls=%async_computation.1 | async-start | bytes 65536 | tf_op jit(solution)/shard_map/all_to_all | solution.py:55
  236.8 43.4 %all-to-all-start.2 = ((f32[8,1,512]{2,1,0:T(1,128)}), f32[8,1,512]{2,1,0:T(1,128)S(1)}, u32[]{:S(2)}, u32[]{:S(2)}) async-start(f32[8,1,512]{2,1,0:T(1,128)} %reshape.1410), calls=%async_computation.2 | async-start | bytes 32768 | tf_op jit(solution)/shard_map/all_to_all | solution.py:116
  280.2 12.7 %all-to-all-start.5 = ((f32[8,1,512]{2,1,0:T(1,128)}), f32[8,1,512]{2,1,0:T(1,128)}, u32[]{:S(2)}, u32[]{:S(2)}) async-start(f32[8,1,512]{2,1,0:T(1,128)} %reshape.1412), calls=%async_computation.5 | async-start | bytes 32768 | tf_op jit(solution)/shard_map/all_to_all | solution.py:116
  303.7 23.1 %all-to-all-start.6 = ((bf16[8,2,256]{2,1,0:T(2,128)(2,1)}), bf16[8,2,256]{2,1,0:T(2,128)(2,1)S(1)}, u32[]{:S(2)}, u32[]{:S(2)}) async-start(bf16[8,2,256]{2,1,0:T(2,128)(2,1)} %reshape.1414), calls=%async_computation.6 | async-start | bytes 16384 | tf_op jit(solution)/shard_map/all_to_all | solution.py:130
  326.8 12.5 %all-to-all-start.9 = ((bf16[8,2,256]{2,1,0:T(2,128)(2,1)}), bf16[8,2,256]{2,1,0:T(2,128)(2,1)S(1)}, u32[]{:S(2)}, u32[]{:S(2)}) async-start(bf16[8,2,256]{2,1,0:T(2,128)(2,1)} %reshape.1416), calls=%async_computation.9 | async-start | bytes 16384 | tf_op jit(solution)/shard_map/all_to_all | solution.py:130
  439.0 49.2 %all-to-all-start.7 = ((bf16[8,8,256]{2,1,0:T(8,128)(2,1)}), bf16[8,8,256]{2,1,0:T(8,128)(2,1)S(1)}, u32[]{:S(2)}, u32[]{:S(2)}) async-start(bf16[8,8,256]{2,1,0:T(8,128)(2,1)} %fusion.138), calls=%async_computation.7 | async-start | bytes 65536 | tf_op jit(solution)/shard_map/all_to_all | solution.py:89
  488.3 12.7 %all-to-all-start.10 = ((bf16[8,8,256]{2,1,0:T(8,128)(2,1)}), bf16[8,8,256]{2,1,0:T(8,128)(2,1)S(1)}, u32[]{:S(2)}, u32[]{:S(2)}) async-start(bf16[8,8,256]{2,1,0:T(8,128)(2,1)} %fusion.139), calls=%async_computation.10 | async-start | bytes 65536 | tf_op jit(solution)/shard_map/all_to_all | solution.py:89
  612.6 89.7 %all-to-all-start.8 = ((bf16[8,8,256]{2,1,0:T(8,128)(2,1)}), bf16[8,8,256]{2,1,0:T(8,128)(2,1)}, u32[]{:S(2)}, u32[]{:S(2)}) async-start(bf16[8,8,256]{2,1,0:T(8,128)(2,1)} %slice_bitcast_fusion.5), calls=%async_computation.8 | async-start | bytes 65536 | tf_op jit(solution)/shard_map/all_to_all | solution.py:79
  659.8 58.6 %copy-start.82 = (f32[64,64]{1,0:T(8,128)S(1)}, f32[64,64]{1,0:T(8,128)}, u32[]{:S(2)}) copy-start(f32[64,64]{1,0:T(8,128)} %param.35) | copy-start | bytes 49156
  659.8 58.6 %copy-start.90 = (f32[64,64]{1,0:T(8,128)S(1)}, f32[64,64]{1,0:T(8,128)}, u32[]{:S(2)}) copy-start(f32[64,64]{1,0:T(8,128)} %param.45) | copy-start | bytes 49156
  659.8 58.6 %copy-start.91 = (f32[64,64]{1,0:T(8,128)S(1)}, f32[64,64]{1,0:T(8,128)}, u32[]{:S(2)}) copy-start(f32[64,64]{1,0:T(8,128)} %param.40) | copy-start | bytes 49156
  660.1 184.1 %copy-start.48 = (f32[128,768]{0,1:T(8,128)S(1)}, f32[128,768]{0,1:T(8,128)}, u32[]{:S(2)}) copy-start(f32[128,768]{0,1:T(8,128)} %copy.427) | copy-start | bytes 1179652
  660.1 184.1 %copy-start.49 = (f32[128,768]{0,1:T(8,128)S(1)}, f32[128,768]{0,1:T(8,128)}, u32[]{:S(2)}) copy-start(f32[128,768]{0,1:T(8,128)} %copy.425) | copy-start | bytes 1179652
  660.1 184.0 %copy-start.50 = (f32[128,768]{0,1:T(8,128)S(1)}, f32[128,768]{0,1:T(8,128)}, u32[]{:S(2)}) copy-start(f32[128,768]{0,1:T(8,128)} %copy.392) | copy-start | bytes 1179652
  702.3 12.0 %all-to-all-start.11 = ((bf16[8,8,256]{2,1,0:T(8,128)(2,1)}), bf16[8,8,256]{2,1,0:T(8,128)(2,1)S(1)}, u32[]{:S(2)}, u32[]{:S(2)}) async-start(bf16[8,8,256]{2,1,0:T(8,128)(2,1)} %slice_bitcast_fusion.4), calls=%async_computation.11 | async-start | bytes 65536 | tf_op jit(solution)/shard_map/all_to_all | solution.py:79
  707.6 136.6 %all-reduce.4.cloned.1.call-start = ((), (), s32[]{:S(2)}) async-start(), calls=%async_computation.12 | async-start | bytes 1966080 | tf_op jit(solution)/shard_map/psum | solution.py:213
  718.4 130.5 %copy-start.32 = (f32[256,576]{0,1:T(8,128)S(1)}, f32[256,576]{0,1:T(8,128)}, u32[]{:S(2)}) copy-start(f32[256,576]{0,1:T(8,128)} %param.34) | copy-start | bytes 1769476
  (127 other events, 1575.2 us)
Sparse Core Ops, SparseCore 0:
  716.0 128.1 all-reduce.3
where the time goes:
time: 868 us; the launch traced here: 859 us
  local copies, waits for them, and re-layouts  310 us (36%)
  other arithmetic  265 us (31%)
  waiting for transfers between devices  141 us (16%)
  starting transfers between devices  66.1 us (8%)
  blocking collectives  41.4 us (5%)
  between operations  18.5 us (2%)
  matrix products  17.6 us (2%)
    psum x1, waiting for transfers between devices, body(): lax.psum((grads[0], grads[1], grads[2], grads[3], grads[4], loss_local, c...  124 us
    scatter-add x4, other arithmetic, layer_backward(): jnp.zeros(table.shape, jnp.float32).at[edges.reshape(-1)]  61.4 us
    broadcast_in_dim x12, local copies, waits for them, and re-layouts, attend(): score = jnp.sum((mixed * vecs[0]).reshape(rows, FAN, HEADS, -1), axis=-1)  52.2 us
    mul x8, local copies, waits for them, and re-layouts, attend(): alpha[..., None] * gathered.reshape(rows, FAN, HEADS, -1)  49.2 us
    reduce_sum x4, other arithmetic, attend(): score = jnp.sum((mixed * vecs[0]).reshape(rows, FAN, HEADS, -1), axis=-1)  45.4 us
    psum x1, blocking collectives, body(): lax.psum((grads[0], grads[1], grads[2], grads[3], grads[4], loss_local, c...  41.4 us
    convert_element_type x8, local copies, waits for them, and re-layouts, layer_forward(): table[edges].astype(jnp.float32)  33.6 us
    gather x4, local copies, waits for them, and re-layouts, layer_forward(): table[edges].astype(jnp.float32)  31.4 us
  transfers between devices with their start and end apart: 13, of which 5 were waited for; matrix products, arithmetic and copies ran while one was open for 28% of the time, Pallas kernels for 0%

commit v1 on v0

v1 whole, which is shorter than its diff:
```python
import functools
from types import SimpleNamespace

import jax
import jax.numpy as jnp
from jax import lax
from jax.experimental import pallas as pl
from jax.experimental.pallas import tpu as pltpu
from jax.sharding import PartitionSpec as P

HEADS = 4
STEP = 5
LANES = 128

eps_norm = 1e-05
beta_one = 0.9
beta_two = 0.999
rate_step = 0.05
decay_rate = 0.01
eps_adam = 1e-08

F32 = jnp.float32
BF16 = jnp.bfloat16
MESH = pl.DeviceIdType.MESH


def contract(left, right, left_dim, right_dim):
    return lax.dot_general(
        left, right, (((left_dim,), (right_dim,)), ((), ())), preferred_element_type=F32
    )


def nn(left, right):
    return contract(left, right, 1, 0)


def nt(left, right):
    return contract(left, right, 1, 1)


def tn(left, right):
    return contract(left, right, 0, 0)


def split(value):
    high = value.astype(BF16)
    return high, (value - high.astype(F32)).astype(BF16)


def sigmoid(value):
    return 0.5 * jnp.tanh(0.5 * value) + 0.5


def row_iota(rows, columns):
    return lax.broadcasted_iota(jnp.int32, (rows, columns), 0)


def lane_iota(rows, columns):
    return lax.broadcasted_iota(jnp.int32, (rows, columns), 1)


def aligned(index, size):
    return pl.ds(pl.multiple_of(index * size, size), size)


def step_kernel(dims, names, *refs):
    (feats, edges, degree, sends, psrc, pdst, plive, w1, w2, wh, vec, bias, gbig, gsmall) = refs[:14]
    s = SimpleNamespace(**dict(zip(names, refs[14:])))
    nd, nr, mb, nodes, fan, hid, head, ext, halo, pairs, rows_all = dims
    half = pairs // 2
    tiles = nodes // LANES
    me = lax.axis_index("dom")
    mine = lax.axis_index("rep")
    rep_rows = rows_all // nr
    dom_rows = rep_rows // nd

    def peers(axis, index, count, send):
        def one(step, carry):
            send(lax.rem(index + step, count))
            return carry

        lax.fori_loop(1, count, one, 0)

    def push(axis, peer, src, dst, send_sem, recv_sem):
        pltpu.make_async_remote_copy(
            src_ref=src,
            dst_ref=dst,
            send_sem=send_sem,
            recv_sem=recv_sem,
            device_id={axis: peer},
            device_id_type=MESH,
        ).start()

    def arrived(ref, sem):
        pltpu.make_async_copy(ref, ref, sem).wait()

    def scatter_out(src, dst, number):
        send_sem, recv_sem = s.send_sems.at[number], s.recv_sems.at[number]
        peers(
            "dom",
            me,
            nd,
            lambda peer: push("dom", peer, src.at[peer], dst.at[me], send_sem, recv_sem),
        )
        pltpu.make_async_copy(src.at[me], dst.at[me], recv_sem).start()

    barrier = pltpu.get_barrier_semaphore()
    peers(
        "dom",
        me,
        nd,
        lambda peer: pl.semaphore_signal(barrier, inc=1, device_id={"dom": peer}, device_id_type=MESH),
    )
    peers(
        "rep",
        mine,
        nr,
        lambda peer: pl.semaphore_signal(barrier, inc=1, device_id={"rep": peer}, device_id_type=MESH),
    )

    for b in range(mb):
        spread = (
            lax.div(row_iota(halo, nd), halo // nd) == lane_iota(halo, nd)
        ).astype(F32).astype(BF16)
        listed = nn(spread, sends[b].astype(F32).astype(BF16))
        pick = lax.rem(row_iota(halo, halo // nd), halo // nd) == lane_iota(halo, halo // nd)
        column = jnp.sum(jnp.where(pick, listed, 0.0), axis=1, keepdims=True)
        s.ohs[b] = (lane_iota(halo, nodes).astype(F32) == column).astype(F32).astype(BF16)
        s.fext[b, :nodes, :] = feats[b].astype(BF16)

    parts = [
        nn(s.ohs[b], s.fext[b, :nodes, :]).reshape(nd, halo // nd, LANES) for b in range(mb)
    ]
    s.fsend[...] = jnp.concatenate(parts, axis=1).astype(BF16)
    pl.semaphore_wait(barrier, nd + nr - 2)
    scatter_out(s.fsend, s.frecv, 0)

    s.w1t[...] = w1[...].T.astype(BF16)
    s.w2b[...] = w2[...].astype(BF16)
    s.w2t[: 2 * hid, :] = w2[:, : 2 * hid].T.astype(BF16)
    s.w2t[2 * hid :, :] = w2[:, 2 * hid :].T.astype(BF16)
    whb = wh[...].astype(BF16)
    for j in range(5):
        s.vb[j] = jnp.broadcast_to(vec[j : j + 1, :], (LANES, hid)).T
    s.bb[...] = jnp.broadcast_to(bias[0:1, :], (LANES, head)).T
    s.acc[...] = jnp.zeros_like(s.acc)
    s.accb[...] = jnp.zeros_like(s.accb)
    s.sm[...] = jnp.zeros_like(s.sm)
    s.tmp[...] = jnp.zeros_like(s.tmp)

    for b in range(mb):
        s.tmp[:, :fan] = edges[b].astype(F32)
        s.et[b] = s.tmp[...].T[:16, :]

        def one_hot(k, carry):
            index = s.et[b, pl.ds(k, 1), :]
            s.oht[b, :, aligned(k, nodes)] = (
                (row_iota(ext, nodes).astype(F32) == index).astype(F32).astype(BF16)
            )
            return carry

        lax.fori_loop(0, fan, one_hot, 0)

        rest = nt(s.w1t[hid:, :], s.fext[b, :nodes, :])
        s.tgt[0, b] = rest[:hid]
        s.res1[b] = rest[hid:]

        slot = lax.rem(lane_iota(1, pairs), half)
        live = slot < plive[b : b + 1, :]
        from_src = (row_iota(nodes, pairs) == psrc[b : b + 1, :]).astype(F32).astype(BF16)
        to_dst = (
            ((row_iota(ext, pairs) == pdst[b : b + 1, :]) & live).astype(F32).astype(BF16)
        )
        s.cpos[b] = nt(from_src[:, :half], to_dst[:, :half])
        s.cneg[b] = nt(from_src[:, half:], to_dst[:, half:])

    def place(index):
        tile, which = lax.div(index, HEADS), lax.rem(index, HEADS)
        return tile, which, aligned(which, head), aligned(tile, LANES)

    def slot_at(k, tile):
        return pl.ds(pl.multiple_of(k * nodes + tile * LANES, LANES), LANES)

    def gather_rows(layer, b):
        def one(k, carry):
            s.g[layer, b, :, aligned(k, nodes)] = nn(s.tab[b], s.oht[b, :, aligned(k, nodes)])
            return carry

        lax.fori_loop(0, fan, one, 0)

    def attend(layer, b):
        att = 0 if layer == 0 else 4
        gather_rows(layer, b)

        def one(index, carry):
            tile, which, rows, cols = place(index)
            target = s.tgt[layer, b, rows, cols]
            weight = s.vb[att, rows, :]
            count = degree[b : b + 1, cols]
            scores = []
            for k in range(fan):
                u = s.g[layer, b, rows, slot_at(k, tile)] + target
                mixed = u * sigmoid(u)
                score = jnp.sum(mixed * weight, axis=0, keepdims=True)
                scores.append(jnp.where(count > k, score, -1e30))
            top = functools.reduce(jnp.maximum, scores)
            weights = [
                jnp.where(count > k, jnp.exp(scores[k] - top), 0.0) for k in range(fan)
            ]
            inverse = 1.0 / functools.reduce(jnp.add, weights)
            message = jnp.zeros((head, LANES), F32)
            for k in range(fan):
                alpha = weights[k] * inverse
                s.al[layer, b, index, k : k + 1, :] = alpha
                message = message + alpha * s.g[layer, b, rows, slot_at(k, tile)]
            s.msg[rows, cols] = message
            return carry

        lax.fori_loop(0, tiles * HEADS, one, 0)

    def attend_back(layer, b):
        att = 0 if layer == 0 else 4

        def one(index, carry):
            tile, which, rows, cols = place(index)
            target = s.tgt[layer, b, rows, cols]
            weight = s.vb[att, rows, :]
            if layer == 0:
                d_message = s.dmsg[rows, cols]
            else:
                d_message = s.dmsg[:head, cols]
            alphas = [s.al[layer, b, index, k : k + 1, :] for k in range(fan)]
            d_alphas = [
                jnp.sum(d_message * s.g[layer, b, rows, slot_at(k, tile)], axis=0, keepdims=True)
                for k in range(fan)
            ]
            total = functools.reduce(jnp.add, [a * d for a, d in zip(alphas, d_alphas)])
            d_target = jnp.zeros((head, LANES), F32)
            d_att = jnp.zeros((head, LANES), F32)
            for k in range(fan):
                d_score = alphas[k] * (d_alphas[k] - total)
                u = s.g[layer, b, rows, slot_at(k, tile)] + target
                gate = sigmoid(u)
                mixed = u * gate
                slope = gate * (1.0 + (u - mixed))
                d_u = (d_score * weight) * slope
                d_target = d_target + d_u
                d_att = d_att + d_score * mixed
                s.dg[rows, slot_at(k, tile)] = (alphas[k] * d_message + d_u).astype(BF16)
            s.dtgt[rows, cols] = d_target
            s.acc[att, rows, :] += d_att
            return carry

        lax.fori_loop(0, tiles * HEADS, one, 0)

    def pack_rows(value):
        blocks = value.reshape(nd, halo // nd, hid)
        return jnp.concatenate([blocks[:, :, :LANES], blocks[:, :, LANES:]], axis=1).astype(BF16)

    def unpack_rows(ref):
        blocks = ref[...].astype(F32)
        per = halo // nd
        return jnp.concatenate([blocks[:, :per, :], blocks[:, per:, :]], axis=2).reshape(halo, hid)

    def layer_one(b):
        s.fext[b, nodes:, :] = (
            s.frecv[...].astype(F32)[:, b * (halo // nd) : (b + 1) * (halo // nd), :]
            .reshape(halo, LANES)
            .astype(BF16)
        )
        s.tab[b] = nt(s.w1t[:hid, :], s.fext[b]).astype(BF16)
        attend(0, b)
        for t in range(tiles):
            cols = slice(t * LANES, (t + 1) * LANES)
            y = s.msg[:, cols] + s.vb[1] + s.res1[b, :, cols]
            centred = y - jnp.sum(y, axis=0, keepdims=True) * (1.0 / hid)
            spread = jnp.sum(centred * centred, axis=0, keepdims=True) * (1.0 / hid)
            rstd = lax.rsqrt(spread + eps_norm)
            normed = centred * rstd
            s.xhat[b, :, cols] = normed
            s.rstd[b, 0:1, cols] = rstd
            n = normed * s.vb[2] + s.vb[3]
            s.h1t[b, :, cols] = jnp.where(n > 0.0, n, jnp.exp(jnp.minimum(n, 0.0)) - 1.0).astype(BF16)
        s.hsend[b] = pack_rows(nt(s.ohs[b], s.h1t[b]))
        scatter_out(s.hsend.at[b], s.hrecv.at[b], 1 + b)
        own = nn(s.w2t[...], s.h1t[b])
        s.own2[b] = own[:hid].astype(BF16)
        s.tgt[1, b] = own[hid : 2 * hid]
        s.res2[b] = own[2 * hid :]

    def layer_two(b):
        arrived(s.hrecv.at[b], s.recv_sems.at[1 + b])
        s.tab[b, :, :nodes] = s.own2[b]
        s.tab[b, :, nodes:] = nt(s.w2t[:hid, :], unpack_rows(s.hrecv.at[b]).astype(BF16)).astype(BF16)
        attend(1, b)
        for t in range(tiles):
            cols = slice(t * LANES, (t + 1) * LANES)
            message = functools.reduce(
                jnp.add, [s.msg[h * head : (h + 1) * head, cols] for h in range(HEADS)]
            )
            s.h2[:, cols] = message * (1.0 / HEADS) + s.bb[...] + s.res2[b, :, cols]
        s.h2t[b] = s.h2[...].astype(BF16)
        rows = nt(s.ohs[b], s.h2t[b])
        s.zsend[b, :, :, :head] = rows.reshape(nd, halo // nd, head)
        scatter_out(s.zsend.at[b], s.zrecv.at[b], 3 + b)
        s.h2r[b, :nodes, :] = s.h2[...].T.astype(BF16)

    def pair_loss(b):
        arrived(s.zrecv.at[b], s.recv_sems.at[3 + b])
        s.h2r[b, nodes:, :] = s.zrecv[b].reshape(halo, LANES)[:, :head].astype(BF16)
        z = nn(s.h2r[b], whb) + bias[1:2, :]
        high, low = split(z)
        left = jnp.concatenate([high[:nodes], high[:nodes], low[:nodes]], axis=1)
        right = jnp.concatenate([high, low, high], axis=1)
        score = nt(left, right)
        pos, neg = s.cpos[b], s.cneg[b]
        small = jnp.exp(-jnp.abs(score))
        terms = (
            (pos + neg) * jnp.log1p(small)
            + pos * jnp.maximum(-score, 0.0)
            + neg * jnp.maximum(score, 0.0)
        )
        s.sm[12:13, 0:1] += jnp.sum(jnp.sum(terms, axis=0, keepdims=True), axis=1, keepdims=True)
        big = 1.0 / (1.0 + small)
        little = small * big
        up = score > 0.0
        d_score = neg * jnp.where(up, big, little) - pos * jnp.where(up, little, big)
        d_low = d_score.astype(BF16)
        d_table = tn(d_low, high[:nodes])
        s.dz[b] = nn(d_low, high) + d_table[:nodes]
        s.ysend[b, :, :, :head] = d_table[nodes:].reshape(nd, halo // nd, head)
        scatter_out(s.ysend.at[b], s.yrecv.at[b], 5 + b)

    def add_to(ref, value, b):
        if b == 0:
            ref[...] = value
        else:
            ref[...] += value

    def back_two(b):
        arrived(s.yrecv.at[b], s.recv_sems.at[5 + b])
        returned = s.yrecv[b].reshape(halo, LANES)[:, :head].astype(BF16)
        dz = s.dz[b] + tn(s.ohs[b], returned)
        s.sm[11:12, :head] += jnp.sum(dz, axis=0, keepdims=True)
        dz_low = dz.astype(BF16)
        add_to(s.gwh, nn(s.h2t[b], dz_low), b)
        d_out = nt(whb, dz_low)
        s.dres2[b] = d_out.astype(BF16)
        s.dmsg[:head, :] = d_out * (1.0 / HEADS)
        s.accb[...] += functools.reduce(
            jnp.add, [d_out[:, t * LANES : (t + 1) * LANES] for t in range(tiles)]
        )
        attend_back(1, b)
        s.dproj2[b, hid : 2 * hid, :] = s.dtgt[...].astype(BF16)
        s.dproj2[b, 2 * hid :, :] = s.dres2[b]
        s.gsend[b] = pack_rows(nt(s.oht[b, nodes:, :], s.dg[...]))
        scatter_out(s.gsend.at[b], s.grecv.at[b], 7 + b)
        s.dsrc[b] = nt(s.dg[...], s.oht[b, :nodes, :])

    def finish_two(b):
        arrived(s.grecv.at[b], s.recv_sems.at[7 + b])
        returned = unpack_rows(s.grecv.at[b]).astype(BF16)
        s.dproj2[b, :hid, :] = (s.dsrc[b] + tn(returned, s.ohs[b])).astype(BF16)
        add_to(s.gw2, nt(s.dproj2[b], s.h1t[b]), b)
        s.dh[...] = nn(s.w2b[...], s.dproj2[b])

    def back_one(b):
        for t in range(tiles):
            cols = slice(t * LANES, (t + 1) * LANES)
            normed = s.xhat[b, :, cols]
            n = normed * s.vb[2] + s.vb[3]
            dn = s.dh[:, cols] * jnp.where(n > 0.0, 1.0, jnp.exp(jnp.minimum(n, 0.0)))
            s.acc[3] += dn
            s.acc[2] += dn * normed
            dx = dn * s.vb[2]
            mean = jnp.sum(dx, axis=0, keepdims=True) * (1.0 / hid)
            along = jnp.sum(dx * normed, axis=0, keepdims=True) * (1.0 / hid)
            dy = s.rstd[b, 0:1, cols] * (dx - mean - normed * along)
            s.acc[1] += dy
            s.dmsg[:, cols] = dy
        attend_back(0, b)
        d_table = nt(s.dg[...], s.oht[b]).astype(BF16)
        d_rest = jnp.concatenate([s.dtgt[...], s.dmsg[...]], axis=0).astype(BF16)
        d_source = nn(d_table, s.fext[b])
        d_other = nn(d_rest, s.fext[b, :nodes, :])
        add_to(s.gw1.at[:hid, :], d_source, b)
        add_to(s.gw1.at[hid:, :], d_other, b)

    s.zsend[...] = jnp.zeros_like(s.zsend)
    s.ysend[...] = jnp.zeros_like(s.ysend)
    arrived(s.frecv, s.recv_sems.at[0])
    for stage in (layer_one, layer_two, pair_loss, back_two):
        for b in range(mb):
            stage(b)
    for b in range(mb):
        finish_two(b)
        back_one(b)

    in_one, in_two = 3 * hid, 2 * hid + head
    s.gb[:in_one, :] = s.gw1[...].astype(BF16)
    s.gb[in_one : in_one + in_two, :] = s.gw2[:, :LANES].astype(BF16)
    s.gb[in_one + in_two : in_one + 2 * in_two, :] = s.gw2[:, LANES:].astype(BF16)
    last = in_one + 2 * in_two
    s.gb[last:, :] = jnp.zeros((rows_all - last, LANES), BF16)
    s.gb[last : last + head, :head] = s.gwh[...].astype(BF16)
    for j in range(5):
        total = jnp.sum(s.acc[j].T, axis=0, keepdims=True)
        s.sm[2 * j : 2 * j + 1, :] = total[:, :LANES]
        s.sm[2 * j + 1 : 2 * j + 2, :] = total[:, LANES:]
    s.sm[10:11, :head] = jnp.sum(s.accb[...].T, axis=0, keepdims=True)
    s.sm[13:14, 0:1] = 2.0 * jnp.sum(plive[...].astype(F32), axis=0, keepdims=True)

    def part(ref, index, count):
        return ref.at[aligned(index, count), :]

    peers(
        "rep",
        mine,
        nr,
        lambda peer: push(
            "rep", peer, part(s.gb, peer, rep_rows), s.rb.at[mine], s.send_sems.at[9], s.recv_sems.at[9]
        ),
    )
    peers(
        "rep",
        mine,
        nr,
        lambda peer: push("rep", peer, s.sm, s.sm1.at[mine], s.send_sems.at[10], s.recv_sems.at[10]),
    )
    pltpu.make_async_copy(part(s.gb, mine, rep_rows), s.rb.at[mine], s.recv_sems.at[9]).start()
    pltpu.make_async_copy(s.sm, s.sm1.at[mine], s.recv_sems.at[10]).start()
    arrived(s.sm1, s.recv_sems.at[10])
    s.sms[...] = functools.reduce(jnp.add, [s.sm1[i] for i in range(nr)])
    peers(
        "dom",
        me,
        nd,
        lambda peer: push("dom", peer, s.sms, s.sm2.at[me], s.send_sems.at[11], s.recv_sems.at[11]),
    )
    pltpu.make_async_copy(s.sms, s.sm2.at[me], s.recv_sems.at[11]).start()
    arrived(s.rb, s.recv_sems.at[9])
    s.gd[...] = functools.reduce(jnp.add, [s.rb[i].astype(F32) for i in range(nr)]).astype(BF16)
    peers(
        "dom",
        me,
        nd,
        lambda peer: push(
            "dom", peer, part(s.gd, peer, dom_rows), s.rd.at[me], s.send_sems.at[12], s.recv_sems.at[12]
        ),
    )
    pltpu.make_async_copy(part(s.gd, me, dom_rows), s.rd.at[me], s.recv_sems.at[12]).start()
    arrived(s.rd, s.recv_sems.at[12])
    s.fin[...] = functools.reduce(jnp.add, [s.rd[i].astype(F32) for i in range(nd)]).astype(BF16)
    place_mine = s.ag.at[mine, me]
    peers(
        "dom",
        me,
        nd,
        lambda peer: push("dom", peer, s.fin, place_mine, s.send_sems.at[13], s.recv_sems.at[13]),
    )
    pltpu.make_async_copy(s.fin, place_mine, s.recv_sems.at[13]).start()
    arrived(s.ag.at[mine], s.recv_sems.at[13])
    peers(
        "rep",
        mine,
        nr,
        lambda peer: push(
            "rep", peer, s.ag.at[mine], s.ag.at[mine], s.send_sems.at[14], s.recv_sems.at[14]
        ),
    )
    arrived(s.sm2, s.recv_sems.at[11])
    gsmall[...] = functools.reduce(jnp.add, [s.sm2[i] for i in range(nd)])
    arrived(s.ag.at[pl.ds(0, nr - 1)], s.recv_sems.at[14])
    gbig[...] = s.ag[...].reshape(rows_all, LANES)

    arrived(s.fsend.at[pl.ds(0, nd - 1)], s.send_sems.at[0])
    for first, ref in ((1, s.hsend), (3, s.zsend), (5, s.ysend), (7, s.gsend)):
        for b in range(mb):
            arrived(ref.at[b, pl.ds(0, nd - 1)], s.send_sems.at[first + b])
    arrived(s.rb.at[pl.ds(0, nr - 1)], s.send_sems.at[9])
    arrived(s.sm1.at[pl.ds(0, nr - 1)], s.send_sems.at[10])
    arrived(s.sm2.at[pl.ds(0, nd - 1)], s.send_sems.at[11])
    arrived(s.rd.at[pl.ds(0, nd - 1)], s.send_sems.at[12])
    arrived(s.rd.at[pl.ds(0, nd - 1)], s.send_sems.at[13])
    arrived(s.ag.at[pl.ds(0, nr - 1)], s.send_sems.at[14])


def adamw(param, grad, first, second):
    first = beta_one * first + (1.0 - beta_one) * grad
    second = beta_two * second + (1.0 - beta_two) * grad * grad
    fhat = first * (1.0 / (1.0 - beta_one**STEP))
    shat = second * (1.0 / (1.0 - beta_two**STEP))
    return (
        first,
        second,
        param - rate_step * (fhat / (jnp.sqrt(shat) + eps_adam) + decay_rate * param),
    )


def adamw_kernel(hid, head, gbig, gsmall, *refs):
    params, firsts, seconds, outs = refs[:5], refs[5:10], refs[10:15], refs[15:]
    loss, count = outs[:2]
    outs = outs[2:]
    loss[...] = gsmall[12:13, 0:1]
    total = gsmall[13:14, 0:1]
    count[...] = total
    scale = 1.0 / total

    def update(index, grad, rows=slice(None), cols=slice(None)):
        made = adamw(
            params[index][rows, cols], grad, firsts[index][rows, cols], seconds[index][rows, cols]
        )
        for offset in range(3):
            outs[3 * index + offset][rows, cols] = made[offset]

    in_one, in_two = 3 * hid, 2 * hid + head
    for c in range(in_one // LANES):
        cols = slice(c * LANES, (c + 1) * LANES)
        update(0, gbig[cols, :].astype(F32).T * scale, slice(None), cols)
    for r in range(hid // LANES):
        rows = slice(r * LANES, (r + 1) * LANES)
        for c in range(0, in_two, LANES):
            width = min(LANES, in_two - c)
            start = in_one + r * in_two + c
            update(
                1, gbig[start : start + width, :].astype(F32).T * scale, rows, slice(c, c + width)
            )
    last = in_one + (hid // LANES) * in_two
    update(2, gbig[last : last + head, :].astype(F32)[:, :head] * scale)
    for j in range(5):
        for p in range(hid // LANES):
            row = (hid // LANES) * j + p
            update(
                3, gsmall[row : row + 1, :] * scale, slice(j, j + 1), slice(p * LANES, (p + 1) * LANES)
            )
    for j in range(2):
        update(4, gsmall[10 + j : 11 + j, :head] * scale, slice(j, j + 1))


def body(nd, nr, *args):
    data, weights, firsts, seconds = args[:7], args[7:12], args[12:17], args[17:]
    features, edge_src, node_degree, send_rows, pair_src, pair_dst, pair_live = (
        a.reshape(a.shape[1:]) for a in data
    )
    mb, nodes, width = features.shape
    fan = edge_src.shape[-1]
    per = send_rows.shape[-1]
    halo = nd * per
    ext = nodes + halo
    pairs = pair_src.shape[-1]
    hid = weights[3].shape[1]
    head = weights[2].shape[0]
    in_one, in_two = 3 * hid, 2 * hid + head
    unit = nd * nr * 16
    rows_all = -(-(in_one + 2 * in_two + head) // unit) * unit
    dims = (nd, nr, mb, nodes, fan, hid, head, ext, halo, pairs, rows_all)
    rep_rows = rows_all // nr
    dom_rows = rep_rows // nd
    scratch = dict(
        ohs=pltpu.VMEM((mb, halo, nodes), BF16),
        fext=pltpu.VMEM((mb, ext, width), BF16),
        fsend=pltpu.VMEM((nd, mb * per, LANES), BF16),
        frecv=pltpu.VMEM((nd, mb * per, LANES), BF16),
        w1t=pltpu.VMEM((in_one, width), BF16),
        w2b=pltpu.VMEM((hid, in_two), BF16),
        w2t=pltpu.VMEM((in_two, hid), BF16),
        vb=pltpu.VMEM((5, hid, LANES), F32),
        bb=pltpu.VMEM((head, LANES), F32),
        acc=pltpu.VMEM((5, hid, LANES), F32),
        accb=pltpu.VMEM((head, LANES), F32),
        sm=pltpu.VMEM((16, LANES), F32),
        tmp=pltpu.VMEM((nodes, LANES), F32),
        et=pltpu.VMEM((mb, 16, nodes), F32),
        oht=pltpu.VMEM((mb, ext, fan * nodes), BF16),
        tgt=pltpu.VMEM((2, mb, hid, nodes), F32),
        res1=pltpu.VMEM((mb, hid, nodes), F32),
        res2=pltpu.VMEM((mb, head, nodes), F32),
        cpos=pltpu.VMEM((mb, nodes, ext), F32),
        cneg=pltpu.VMEM((mb, nodes, ext), F32),
        tab=pltpu.VMEM((mb, hid, ext), BF16),
        g=pltpu.VMEM((2, mb, hid, fan * nodes), F32),
        al=pltpu.VMEM((2, mb, (nodes // LANES) * HEADS, 16, LANES), F32),
        msg=pltpu.VMEM((hid, nodes), F32),
        xhat=pltpu.VMEM((mb, hid, nodes), F32),
        rstd=pltpu.VMEM((mb, 8, nodes), F32),
        h1t=pltpu.VMEM((mb, hid, nodes), BF16),
        hsend=pltpu.VMEM((mb, nd, 2 * per, LANES), BF16),
        hrecv=pltpu.VMEM((mb, nd, 2 * per, LANES), BF16),
        own2=pltpu.VMEM((mb, hid, nodes), BF16),
        h2=pltpu.VMEM((head, nodes), F32),
        h2t=pltpu.VMEM((mb, head, nodes), BF16),
        h2r=pltpu.VMEM((mb, ext, head), BF16),
        zsend=pltpu.VMEM((mb, nd, per, LANES), F32),
        zrecv=pltpu.VMEM((mb, nd, per, LANES), F32),
        ysend=pltpu.VMEM((mb, nd, per, LANES), F32),
        yrecv=pltpu.VMEM((mb, nd, per, LANES), F32),
        dz=pltpu.VMEM((mb, nodes, head), F32),
        dmsg=pltpu.VMEM((hid, nodes), F32),
        dres2=pltpu.VMEM((mb, head, nodes), BF16),
        dtgt=pltpu.VMEM((hid, nodes), F32),
        dg=pltpu.VMEM((hid, fan * nodes), BF16),
        dproj2=pltpu.VMEM((mb, in_two, nodes), BF16),
        dsrc=pltpu.VMEM((mb, hid, nodes), F32),
        gsend=pltpu.VMEM((mb, nd, 2 * per, LANES), BF16),
        grecv=pltpu.VMEM((mb, nd, 2 * per, LANES), BF16),
        dh=pltpu.VMEM((hid, nodes), F32),
        gw1=pltpu.VMEM((in_one, LANES), F32),
        gw2=pltpu.VMEM((in_two, hid), F32),
        gwh=pltpu.VMEM((head, head), F32),
        gb=pltpu.VMEM((rows_all, LANES), BF16),
        rb=pltpu.VMEM((nr, rep_rows, LANES), BF16),
        gd=pltpu.VMEM((rep_rows, LANES), BF16),
        rd=pltpu.VMEM((nd, dom_rows, LANES), BF16),
        fin=pltpu.VMEM((dom_rows, LANES), BF16),
        ag=pltpu.VMEM((nr, nd, dom_rows, LANES), BF16),
        sm1=pltpu.VMEM((nr, 16, LANES), F32),
        sms=pltpu.VMEM((16, LANES), F32),
        sm2=pltpu.VMEM((nd, 16, LANES), F32),
        send_sems=pltpu.SemaphoreType.DMA((15,)),
        recv_sems=pltpu.SemaphoreType.DMA((15,)),
    )
    whole = pl.BlockSpec(memory_space=pltpu.VMEM)
    gbig, gsmall = pl.pallas_call(
        functools.partial(step_kernel, dims, tuple(scratch)),
        out_shape=(
            jax.ShapeDtypeStruct((rows_all, LANES), BF16),
            jax.ShapeDtypeStruct((16, LANES), F32),
        ),
        in_specs=[whole] * 12,
        out_specs=(whole, whole),
        scratch_shapes=list(scratch.values()),
        compiler_params=pltpu.CompilerParams(
            collective_id=0, has_side_effects=True, vmem_limit_bytes=48 * 1024 * 1024
        ),
    )(features, edge_src, node_degree, send_rows, pair_src, pair_dst, pair_live, *weights)

    shapes = [jax.ShapeDtypeStruct((1, 1), F32)] * 2
    for weight in weights:
        shapes += [jax.ShapeDtypeStruct(weight.shape, F32)] * 3
    made = pl.pallas_call(
        functools.partial(adamw_kernel, hid, head),
        out_shape=tuple(shapes),
        in_specs=[whole] * 17,
        out_specs=tuple([whole] * 17),
        compiler_params=pltpu.CompilerParams(vmem_limit_bytes=32 * 1024 * 1024),
    )(gbig, gsmall, *weights, *firsts, *seconds)
    return (made[0].reshape(()), made[1].reshape(())) + tuple(made[2:])


def solution(mesh):
    sharded = (
        P("rep", None, "dom", None),
        P("rep", None, "dom", None),
        P("rep", None, "dom"),
        P("rep", None, "dom", None),
        P("rep", None, "dom"),
        P("rep", None, "dom"),
        P("rep", None, "dom"),
    )
    return jax.shard_map(
        functools.partial(body, mesh.shape["dom"], mesh.shape["rep"]),
        mesh=mesh,
        in_specs=sharded + (P(),) * 15,
        out_specs=(P(),) * 17,
        check_vma=False,
    )
```

time: 868 us -> 92.5 us (0.11)
  local copies, waits for them, and re-layouts: 310 us -> 19 us
  other arithmetic: 265 us -> 0 us
  waiting for transfers between devices: 141 us -> 0 us
  Pallas kernels: 0 us -> 71.4 us
  starting transfers between devices: 66.1 us -> 0 us
  blocking collectives: 41.4 us -> 0 us
  between operations: 18.5 us -> 0.88 us
  matrix products: 17.6 us -> 0 us
    reduce_sum x34 -> x0, other arithmetic: 126 us -> none  [the longest x4 45.4 us: attend(): score = jnp.sum((mixed * vecs[0]).reshape(rows, FAN, HEADS, -1), axis=-1)]
    psum x1 -> x0, waiting for transfers between devices: 124 us -> none  [body(): lax.psum((grads[0], grads[1], grads[2], grads[3], grads[4], loss_local, c...]
    scatter-add x12 -> x0, other arithmetic: 82.7 us -> none  [the longest x4 61.4 us: layer_backward(): jnp.zeros(table.shape, jnp.float32).at[edges.reshape(-1)]]
    broadcast_in_dim x24 -> x0, local copies, waits for them, and re-layouts: 80.2 us -> none  [the longest x12 52.2 us: attend(): score = jnp.sum((mixed * vecs[0]).reshape(rows, FAN, HEADS, -1), axis=-1)]
    pallas_call x0 -> x2, Pallas kernels: none -> 71.4 us  [the longest x1 69.7 us: body(): pl.pallas_call(functools.partial(step_kernel, dims, tuple(scratch)), out_...]
    all_to_all x12 -> x0, starting transfers between devices: 66 us -> none  [the longest x4 25.8 us: layer_forward(): lax.all_to_all(outgoing, 'dom', split_axis=0, concat_axis=0, tiled=True)]
    mul x10 -> x0, local copies, waits for them, and re-layouts: 49.3 us -> none  [the longest x8 49.2 us: attend(): alpha[..., None] * gathered.reshape(rows, FAN, HEADS, -1)]
    gather x16 -> x0, local copies, waits for them, and re-layouts: 48.2 us -> none  [the longest x4 31.4 us: layer_forward(): table[edges].astype(jnp.float32)]
  transfers between devices with their start and end apart: 13 -> 0, of which waited for: 5 -> 0; matrix products, arithmetic and copies ran while one was open for 28% -> 0% of each run, Pallas kernels for 0% -> 0%
where the time goes in v1:
time: 92.5 us; the launch traced here: 91.3 us
  Pallas kernels  71.4 us (77%)
  local copies, waits for them, and re-layouts  19 us (21%)
    pallas_call x1, Pallas kernels, body(): pl.pallas_call(functools.partial(step_kernel, dims, tuple(scratch)), out_...  69.7 us
    unnamed x61, local copies, waits for them, and re-layouts  18.9 us

profile of v1, /device:TPU:0, one launch (start us, length us, event | category | flops | bytes accessed | tf_op | source)
XLA Modules:
  0.0 91.3 jit_solution(15396122622499513992)
XLA Ops:
  0.7 0.6 copy-done.26
  1.4 0.9 copy.39
  2.4 1.3 %copy.41.refs_8_.refs_1_ = f32[256,576]{1,0:T(8,128)S(1)} copy(f32[256,576]{0,1:T(8,128)} %param.30) | data formatting | bytes 1179648 | tf_op args[8]
  3.8 69.7 %shard_map.341 = (bf16[2048,128]{1,0:T(8,128)(2,1)S(1)}, f32[16,128]{1,0:T(8,128)S(1)}) custom-call(f32[2,256,128]{2,1,0:T(8,128)S(1)} %bitcast.10, s32[2,256,10]{2,1,0:T(8,128)S(1)} %bitcast.9, s32[2,256]{1,0:T(2,128)S(1)} %bitcast.14, s32[2,8,8]{2,1,0:T(8,128)S(1)} %bitcast.11, s32[2,512]{1,0:T(2,128)S(1)} %bitcast.12, s32[2,512]{1,0:T(2,128)S(1)} %bitcast.13, ...), custom_call_target="tpu_custom_call" | custom-call | tf_op jit(solution)/shard_map/pallas_call | solution.py:623
  73.6 0.6 copy-done.15
  74.2 0.2 copy.43.refs_6_
  74.4 0.8 copy-done.25
  75.5 0.5 copy-done.13
  75.9 1.0 %copy-done.4 = f32[128,768]{1,0:T(8,128)S(1)} copy-done((f32[128,768]{1,0:T(8,128)S(1)}, f32[128,768]{1,0:T(8,128)}, u32[]{:S(2)}) %copy-start.4) | copy-done | bytes 393240
  76.9 1.0 %copy-done.5 = f32[128,768]{1,0:T(8,128)S(1)} copy-done((f32[128,768]{1,0:T(8,128)S(1)}, f32[128,768]{1,0:T(8,128)}, u32[]{:S(2)}) %copy-start.5) | copy-done | bytes 393240
  77.9 0.8 copy-done.8
  78.7 0.8 copy-done.9
  79.4 0.8 copy-done.10
  80.2 0.7 copy-done.14
  80.9 0.7 copy-done.16
  81.6 0.7 copy-done.20
  82.3 0.7 copy-done.22
  82.9 0.7 copy-done.23
  83.6 1.7 %shard_map.342 = (f32[1,1]{1,0:T(1,128)}, f32[1,1]{1,0:T(1,128)}, f32[128,768]{1,0:T(8,128)}, f32[128,768]{1,0:T(8,128)}, f32[128,768]{1,0:T(8,128)}, /*index=5*...) custom-call(bf16[2048,128]{1,0:T(8,128)(2,1)S(1)} %get-tuple-element, ...), custom_call_target="tpu_custom_call" | custom-call | tf_op jit(solution)/shard_map/pallas_call | solution.py:640
  85.4 0.8 copy-done.1
  86.2 0.9 copy-done.3
  87.1 2.2 %copy.45 = f32[256,576]{0,1:T(8,128)} copy(f32[256,576]{1,0:T(8,128)} %copy-done.3) | data formatting | bytes 1179648
  89.3 1.0 %copy.46 = f32[256,576]{0,1:T(8,128)} copy(f32[256,576]{1,0:T(8,128)S(1)} %copy-done.2) | data formatting | bytes 1179648
  90.3 1.0 %copy.47 = f32[256,576]{0,1:T(8,128)} copy(f32[256,576]{1,0:T(8,128)S(1)} %get-tuple-element.62) | data formatting | bytes 1179648
  (40 shorter events, 0.4 us)
Async XLA Ops:
  2.3 1.5 %copy-start = (f32[128,768]{1,0:T(8,128)S(1)}, f32[128,768]{1,0:T(8,128)}, u32[]{:S(2)}) copy-start(f32[128,768]{1,0:T(8,128)} %refs_0_.1) | copy-start | bytes 1179652
  2.3 1.5 %copy-start.6 = (f32[1,2,256,128]{3,2,1,0:T(8,128)S(1)}, f32[1,2,256,128]{3,2,1,0:T(8,128)}, u32[]{:S(2)}) copy-start(f32[1,2,256,128]{3,2,1,0:T(8,128)} %param.22) | copy-start | bytes 786436
  2.3 1.5 %copy-start.7 = (f32[64,64]{1,0:T(8,128)S(1)}, f32[64,64]{1,0:T(8,128)}, u32[]{:S(2)}) copy-start(f32[64,64]{1,0:T(8,128)} %refs_2_.1) | copy-start | bytes 49156
  2.3 1.5 %copy-start.11 = (f32[5,256]{1,0:T(8,128)S(1)}, f32[5,256]{1,0:T(8,128)}, u32[]{:S(2)}) copy-start(f32[5,256]{1,0:T(8,128)} %refs_3_.1) | copy-start | bytes 15364
  2.3 1.5 %copy-start.12 = (s32[1,2,8,8]{3,2,1,0:T(8,128)S(1)}, s32[1,2,8,8]{3,2,1,0:T(8,128)}, u32[]{:S(2)}) copy-start(s32[1,2,8,8]{3,2,1,0:T(8,128)} %param.25) | copy-start | bytes 1540
  2.3 1.5 %copy-start.17 = (s32[1,2,512]{2,1,0:T(2,128)S(1)}, s32[1,2,512]{2,1,0:T(2,128)}, u32[]{:S(2)}) copy-start(s32[1,2,512]{2,1,0:T(2,128)} %param.26) | copy-start | bytes 12292
  2.3 1.5 %copy-start.18 = (s32[1,2,512]{2,1,0:T(2,128)S(1)}, s32[1,2,512]{2,1,0:T(2,128)}, u32[]{:S(2)}) copy-start(s32[1,2,512]{2,1,0:T(2,128)} %param.27) | copy-start | bytes 12292
  2.4 1.5 %copy-start.19 = (f32[2,64]{1,0:T(2,128)S(1)}, f32[2,64]{1,0:T(2,128)}, u32[]{:S(2)}) copy-start(f32[2,64]{1,0:T(2,128)} %refs_4_.1) | copy-start | bytes 1540
  2.4 1.4 %copy-start.21 = (s32[1,2,256]{2,1,0:T(2,128)S(1)}, s32[1,2,256]{2,1,0:T(2,128)}, u32[]{:S(2)}) copy-start(s32[1,2,256]{2,1,0:T(2,128)} %param.24) | copy-start | bytes 6148
  3.8 70.3 %copy-start.24 = (f32[256,576]{0,1:T(8,128)S(1)}, f32[256,576]{0,1:T(8,128)}, u32[]{:S(2)}) copy-start(f32[256,576]{0,1:T(8,128)} %param.35) | copy-start | bytes 1769476
  74.2 1.1 %copy-start.25 = (f32[256,576]{0,1:T(8,128)S(1)}, f32[256,576]{0,1:T(8,128)}, u32[]{:S(2)}) copy-start(f32[256,576]{0,1:T(8,128)} %param.40) | copy-start | bytes 1769476
  75.2 0.7 copy-start.13
  75.9 1.0 %copy-start.4 = (f32[128,768]{1,0:T(8,128)S(1)}, f32[128,768]{1,0:T(8,128)}, u32[]{:S(2)}) copy-start(f32[128,768]{1,0:T(8,128)} %refs_5_.1) | copy-start | bytes 1179652
  76.9 1.0 %copy-start.5 = (f32[128,768]{1,0:T(8,128)S(1)}, f32[128,768]{1,0:T(8,128)}, u32[]{:S(2)}) copy-start(f32[128,768]{1,0:T(8,128)} %refs_10_.3) | copy-start | bytes 1179652
  77.9 0.8 copy-start.8
  78.7 0.8 copy-start.9
  79.4 0.8 copy-start.10
  80.2 0.7 copy-start.14
  80.9 0.7 copy-start.16
  81.6 0.7 copy-start.20
  82.9 0.7 copy-start.23
  85.4 0.8 copy-start.1
  86.2 0.9 copy-start.3
  87.1 2.2 %copy-start.2 = (f32[256,576]{1,0:T(8,128)S(1)}, f32[256,576]{1,0:T(8,128)}, u32[]{:S(2)}) copy-start(f32[256,576]{1,0:T(8,128)} %copy-done.1) | copy-start | bytes 1769476
  (3 other events, 1.9 us)

commit v2 on v1

--- a/solution.py
+++ b/solution.py
@@ -64,15 +64,16 @@
 
 
 def step_kernel(dims, names, *refs):
-    (feats, edges, degree, sends, psrc, pdst, plive, w1, w2, wh, vec, bias, gbig, gsmall) = refs[:14]
-    s = SimpleNamespace(**dict(zip(names, refs[14:])))
-    nd, nr, mb, nodes, fan, hid, head, ext, halo, pairs, rows_all = dims
+    held, outs, rest_refs = refs[:22], refs[22:38], refs[38:]
+    staged = rest_refs[:22]
+    s = SimpleNamespace(**dict(zip(names, rest_refs[22:])))
+    (feats, edges, degree, sends, psrc, pdst, plive, w1, w2, wh, vec, bias) = staged[:12]
+    firsts, seconds = staged[12:17], staged[17:22]
+    nd, nr, mb, nodes, fan, hid, head, ext, halo, pairs, bounds = dims
     half = pairs // 2
     tiles = nodes // LANES
     me = lax.axis_index("dom")
     mine = lax.axis_index("rep")
-    rep_rows = rows_all // nr
-    dom_rows = rep_rows // nd
 
     def peers(axis, index, count, send):
         def one(step, carry):
@@ -91,8 +92,27 @@
             device_id_type=MESH,
         ).start()
 
+    incoming, outgoing = {}, []
+
     def arrived(ref, sem):
         pltpu.make_async_copy(ref, ref, sem).wait()
+
+    def receive(number):
+        arrived(incoming.pop(number), s.recv_sems.at[number])
+
+    def finish():
+        for number in list(incoming):
+            receive(number)
+        for number, ref in outgoing:
+            arrived(ref, s.send_sems.at[number])
+
+    def load(*which):
+        for i in which:
+            pltpu.make_async_copy(held[i], staged[i], s.load_sems.at[i]).start()
+
+    def loaded(*which):
+        for i in which:
+            arrived(staged[i], s.load_sems.at[i])
 
     def scatter_out(src, dst, number):
         send_sem, recv_sem = s.send_sems.at[number], s.recv_sems.at[number]
@@ -103,7 +123,10 @@
             lambda peer: push("dom", peer, src.at[peer], dst.at[me], send_sem, recv_sem),
         )
         pltpu.make_async_copy(src.at[me], dst.at[me], recv_sem).start()
-
+        incoming[number] = dst
+        outgoing.append((number, src.at[pl.ds(0, nd - 1)]))
+
+    load(3, 0, 7, 8, 9, 10, 11, 1, 2, 4, 5, 6)
     barrier = pltpu.get_barrier_semaphore()
     peers(
         "dom",
@@ -118,6 +141,8 @@
         lambda peer: pl.semaphore_signal(barrier, inc=1, device_id={"rep": peer}, device_id_type=MESH),
     )
 
+    load(*range(12, 22))
+    loaded(3, 0)
     for b in range(mb):
         spread = (
             lax.div(row_iota(halo, nd), halo // nd) == lane_iota(halo, nd)
@@ -135,10 +160,10 @@
     pl.semaphore_wait(barrier, nd + nr - 2)
     scatter_out(s.fsend, s.frecv, 0)
 
+    loaded(7, 8, 9, 10, 11)
     s.w1t[...] = w1[...].T.astype(BF16)
-    s.w2b[...] = w2[...].astype(BF16)
-    s.w2t[: 2 * hid, :] = w2[:, : 2 * hid].T.astype(BF16)
-    s.w2t[2 * hid :, :] = w2[:, 2 * hid :].T.astype(BF16)
+    s.w2t[...] = w2[...].astype(BF16)
+    s.w2b[...] = w2[...].T.astype(BF16)
     whb = wh[...].astype(BF16)
     for j in range(5):
         s.vb[j] = jnp.broadcast_to(vec[j : j + 1, :], (LANES, hid)).T
@@ -146,16 +171,14 @@
     s.acc[...] = jnp.zeros_like(s.acc)
     s.accb[...] = jnp.zeros_like(s.accb)
     s.sm[...] = jnp.zeros_like(s.sm)
-    s.tmp[...] = jnp.zeros_like(s.tmp)
+    loaded(1, 2, 4, 5, 6)
 
     for b in range(mb):
-        s.tmp[:, :fan] = edges[b].astype(F32)
-        s.et[b] = s.tmp[...].T[:16, :]
 
         def one_hot(k, carry):
-            index = s.et[b, pl.ds(k, 1), :]
+            index = edges[k, b : b + 1, :]
             s.oht[b, :, aligned(k, nodes)] = (
-                (row_iota(ext, nodes).astype(F32) == index).astype(F32).astype(BF16)
+                (row_iota(ext, nodes) == index).astype(F32).astype(BF16)
             )
             return carry
 
@@ -166,7 +189,10 @@
         s.res1[b] = rest[hid:]
 
         slot = lax.rem(lane_iota(1, pairs), half)
-        live = slot < plive[b : b + 1, :]
+        count = jnp.sum(
+            jnp.where(lane_iota(1, mb) == b, plive[...].astype(F32), 0.0), axis=1, keepdims=True
+        )
+        live = slot.astype(F32) < count
         from_src = (row_iota(nodes, pairs) == psrc[b : b + 1, :]).astype(F32).astype(BF16)
         to_dst = (
             ((row_iota(ext, pairs) == pdst[b : b + 1, :]) & live).astype(F32).astype(BF16)
@@ -181,16 +207,9 @@
     def slot_at(k, tile):
         return pl.ds(pl.multiple_of(k * nodes + tile * LANES, LANES), LANES)
 
-    def gather_rows(layer, b):
-        def one(k, carry):
-            s.g[layer, b, :, aligned(k, nodes)] = nn(s.tab[b], s.oht[b, :, aligned(k, nodes)])
-            return carry
-
-        lax.fori_loop(0, fan, one, 0)
-
     def attend(layer, b):
         att = 0 if layer == 0 else 4
-        gather_rows(layer, b)
+        s.g[layer, b] = nn(s.tab[b], s.oht[b])
 
         def one(index, carry):
             tile, which, rows, cols = place(index)
@@ -218,7 +237,7 @@
 
         lax.fori_loop(0, tiles * HEADS, one, 0)
 
-    def attend_back(layer, b):
+    def attend_back(layer, b, first=0, last=None):
         att = 0 if layer == 0 else 4
 
         def one(index, carry):
@@ -251,7 +270,7 @@
             s.acc[att, rows, :] += d_att
             return carry
 
-        lax.fori_loop(0, tiles * HEADS, one, 0)
+        lax.fori_loop(first, tiles * HEADS if last is None else last, one, 0)
 
     def pack_rows(value):
         blocks = value.reshape(nd, halo // nd, hid)
@@ -289,7 +308,7 @@
         s.res2[b] = own[2 * hid :]
 
     def layer_two(b):
-        arrived(s.hrecv.at[b], s.recv_sems.at[1 + b])
+        receive(1 + b)
         s.tab[b, :, :nodes] = s.own2[b]
         s.tab[b, :, nodes:] = nt(s.w2t[:hid, :], unpack_rows(s.hrecv.at[b]).astype(BF16)).astype(BF16)
         attend(1, b)
@@ -306,7 +325,7 @@
         s.h2r[b, :nodes, :] = s.h2[...].T.astype(BF16)
 
     def pair_loss(b):
-        arrived(s.zrecv.at[b], s.recv_sems.at[3 + b])
+        receive(3 + b)
         s.h2r[b, nodes:, :] = s.zrecv[b].reshape(halo, LANES)[:, :head].astype(BF16)
         z = nn(s.h2r[b], whb) + bias[1:2, :]
         high, low = split(z)
@@ -338,7 +357,7 @@
             ref[...] += value
 
     def back_two(b):
-        arrived(s.yrecv.at[b], s.recv_sems.at[5 + b])
+        receive(5 + b)
         returned = s.yrecv[b].reshape(halo, LANES)[:, :head].astype(BF16)
         dz = s.dz[b] + tn(s.ohs[b], returned)
         s.sm[11:12, :head] += jnp.sum(dz, axis=0, keepdims=True)
@@ -358,13 +377,13 @@
         s.dsrc[b] = nt(s.dg[...], s.oht[b, :nodes, :])
 
     def finish_two(b):
-        arrived(s.grecv.at[b], s.recv_sems.at[7 + b])
+        receive(7 + b)
         returned = unpack_rows(s.grecv.at[b]).astype(BF16)
         s.dproj2[b, :hid, :] = (s.dsrc[b] + tn(returned, s.ohs[b])).astype(BF16)
         add_to(s.gw2, nt(s.dproj2[b], s.h1t[b]), b)
         s.dh[...] = nn(s.w2b[...], s.dproj2[b])
 
-    def back_one(b):
+    def norm_back(b):
         for t in range(tiles):
             cols = slice(t * LANES, (t + 1) * LANES)
             normed = s.xhat[b, :, cols]
@@ -378,111 +397,200 @@
             dy = s.rstd[b, 0:1, cols] * (dx - mean - normed * along)
             s.acc[1] += dy
             s.dmsg[:, cols] = dy
-        attend_back(0, b)
+        add_to(s.gw1.at[2 * hid :, :], nn(s.dmsg[...].astype(BF16), s.fext[b, :nodes, :]), b)
+
+    def weights_one(b):
         d_table = nt(s.dg[...], s.oht[b]).astype(BF16)
-        d_rest = jnp.concatenate([s.dtgt[...], s.dmsg[...]], axis=0).astype(BF16)
-        d_source = nn(d_table, s.fext[b])
-        d_other = nn(d_rest, s.fext[b, :nodes, :])
-        add_to(s.gw1.at[:hid, :], d_source, b)
-        add_to(s.gw1.at[hid:, :], d_other, b)
+        add_to(s.gw1.at[:hid, :], nn(d_table, s.fext[b]), b)
+        d_target = nn(s.dtgt[...].astype(BF16), s.fext[b, :nodes, :])
+        add_to(s.gw1.at[hid : 2 * hid, :], d_target, b)
+
+    def part(ref, index, count):
+        return ref.at[aligned(index, count), :]
+
+    def exchange(axis, number, src_of, dst, own=True):
+        index, count = (me, nd) if axis == "dom" else (mine, nr)
+        send_sem, recv_sem = s.send_sems.at[number], s.recv_sems.at[number]
+        peers(
+            axis,
+            index,
+            count,
+            lambda peer: push(axis, peer, src_of(peer), dst.at[index], send_sem, recv_sem),
+        )
+        if own:
+            pltpu.make_async_copy(src_of(index), dst.at[index], recv_sem).start()
+            incoming[number] = dst
+        else:
+            incoming[number] = dst.at[pl.ds(0, count - 1)]
+        outgoing.append((number, dst.at[pl.ds(0, count - 1)]))
+
+    def summed(ref, count):
+        return functools.reduce(jnp.add, [ref[i].astype(F32) for i in range(count)])
+
+    in_one, in_two = 3 * hid, 2 * hid + head
+    regions = [(i * in_two, s.gw2, slice(None), slice(i * LANES, (i + 1) * LANES)) for i in range(hid // LANES)]
+    start = (hid // LANES) * in_two
+    regions.append((start, s.gwh, slice(None), slice(None)))
+    regions.append((start + head, s.gw1, slice(2 * hid, None), slice(None)))
+    regions.append((bounds[-1] - 2 * hid, s.gw1, slice(0, 2 * hid), slice(None)))
+
+    def spans(chunk):
+        low, high = bounds[chunk], bounds[chunk + 1]
+        for at, ref, rows, cols in regions:
+            first, last, _ = rows.indices(ref.shape[0])
+            begin, end = max(low, at), min(high, at + last - first)
+            if begin < end:
+                width = len(range(*cols.indices(ref.shape[1])))
+                yield begin, end, ref, slice(first + begin - at, first + end - at), cols, width
+
+    def pack(chunk):
+        for begin, end, ref, rows, cols, width in spans(chunk):
+            s.gb[begin:end, :width] = ref[rows, cols].astype(BF16)
+
+    def chunk_of(chunk):
+        return [getattr(s, f"{name}{chunk}") for name in ("rb", "gd", "rd", "fin", "ag")]
+
+    def sum_rep(chunk):
+        pack(chunk)
+        low, high = bounds[chunk], bounds[chunk + 1]
+        size = (high - low) // nr
+        here = s.gb.at[low:high, :]
+        exchange("rep", 11 + 4 * chunk, lambda peer: part(here, peer, size), chunk_of(chunk)[0])
+
+    def sum_dom(chunk):
+        rb, gd, rd, fin, ag = chunk_of(chunk)
+        receive(11 + 4 * chunk)
+        gd[...] = summed(rb, nr).astype(BF16)
+        size = gd.shape[0] // nd
+        exchange("dom", 12 + 4 * chunk, lambda peer: part(gd, peer, size), rd)
+
+    def share_dom(chunk):
+        rb, gd, rd, fin, ag = chunk_of(chunk)
+        receive(12 + 4 * chunk)
+        fin[...] = summed(rd, nd).astype(BF16)
+        exchange("dom", 13 + 4 * chunk, lambda peer: fin, ag.at[mine])
+
+    def share_rep(chunk):
+        ag = chunk_of(chunk)[4]
+        receive(13 + 4 * chunk)
+        exchange("rep", 14 + 4 * chunk, lambda peer: ag.at[mine], ag, own=False)
+
+    def vector_sum(j):
+        total = jnp.sum(s.acc[j].T, axis=0, keepdims=True)
+        for p in range(hid // LANES):
+            row = (hid // LANES) * j + p
+            s.sm[row : row + 1, :] = total[:, p * LANES : (p + 1) * LANES]
+
+    def small_rep():
+        exchange("rep", 9, lambda peer: s.sm, s.sm1)
+
+    def small_dom():
+        receive(9)
+        s.sms[...] = summed(s.sm1, nr)
+        exchange("dom", 10, lambda peer: s.sms, s.sm2)
+
+    params = (w1, w2, wh, vec, bias)
+
+    def update(index, grad, rows, cols):
+        made = adamw(
+            params[index][rows, cols], grad, firsts[index][rows, cols], seconds[index][rows, cols]
+        )
+        for offset in range(3):
+            outs[1 + 3 * index + offset][rows, cols] = made[offset]
+
+    def small_update():
+        receive(10)
+        total = summed(s.sm2, nd)
+        outs[0][...] = total
+        scale = 1.0 / total[13:14, 0:1]
+        s.scale[...] = jnp.broadcast_to(scale, s.scale.shape)
+        for j in range(5):
+            for p in range(hid // LANES):
+                row = (hid // LANES) * j + p
+                cols = slice(p * LANES, (p + 1) * LANES)
+                update(3, total[row : row + 1, :] * scale, slice(j, j + 1), cols)
+        for j in range(2):
+            update(4, total[10 + j : 11 + j, :head] * scale, slice(j, j + 1), slice(None))
+
+    def chunk_update(chunk):
+        ag = chunk_of(chunk)[4]
+        receive(14 + 4 * chunk)
+        low, high = bounds[chunk], bounds[chunk + 1]
+        whole = ag[...].reshape(high - low, LANES)
+        scale = s.scale[0:1, 0:1]
+        for begin, end, ref, rows, cols, width in spans(chunk):
+            if ref is s.gw1:
+                for at in range(0, end - begin, LANES):
+                    grad = whole[begin - low + at : begin - low + at + LANES].astype(F32).T * scale
+                    update(0, grad, slice(None), slice(rows.start + at, rows.start + at + LANES))
+            else:
+                grad = whole[begin - low : end - low].astype(F32)[:, :width] * scale
+                update(1 if ref is s.gw2 else 2, grad, rows, cols)
 
     s.zsend[...] = jnp.zeros_like(s.zsend)
     s.ysend[...] = jnp.zeros_like(s.ysend)
-    arrived(s.frecv, s.recv_sems.at[0])
-    for stage in (layer_one, layer_two, pair_loss, back_two):
-        for b in range(mb):
-            stage(b)
+    s.gb[...] = jnp.zeros_like(s.gb)
+    s.sm[13:14, 0:1] = 2.0 * jnp.sum(plive[...].astype(F32), axis=1, keepdims=True)
+    receive(0)
+    stages = [(stage, b) for stage in (layer_one, layer_two, pair_loss, back_two) for b in range(mb)]
+    for stage, b in stages:
+        stage(b)
+
+    chunks = len(bounds) - 1
+    split_sum = chunks == 3
+    middle = tiles * HEADS // 2
     for b in range(mb):
+        final = b == mb - 1
         finish_two(b)
-        back_one(b)
-
-    in_one, in_two = 3 * hid, 2 * hid + head
-    s.gb[:in_one, :] = s.gw1[...].astype(BF16)
-    s.gb[in_one : in_one + in_two, :] = s.gw2[:, :LANES].astype(BF16)
-    s.gb[in_one + in_two : in_one + 2 * in_two, :] = s.gw2[:, LANES:].astype(BF16)
-    last = in_one + 2 * in_two
-    s.gb[last:, :] = jnp.zeros((rows_all - last, LANES), BF16)
-    s.gb[last : last + head, :head] = s.gwh[...].astype(BF16)
-    for j in range(5):
-        total = jnp.sum(s.acc[j].T, axis=0, keepdims=True)
-        s.sm[2 * j : 2 * j + 1, :] = total[:, :LANES]
-        s.sm[2 * j + 1 : 2 * j + 2, :] = total[:, LANES:]
-    s.sm[10:11, :head] = jnp.sum(s.accb[...].T, axis=0, keepdims=True)
-    s.sm[13:14, 0:1] = 2.0 * jnp.sum(plive[...].astype(F32), axis=0, keepdims=True)
-
-    def part(ref, index, count):
-        return ref.at[aligned(index, count), :]
-
-    peers(
-        "rep",
-        mine,
-        nr,
-        lambda peer: push(
-            "rep", peer, part(s.gb, peer, rep_rows), s.rb.at[mine], s.send_sems.at[9], s.recv_sems.at[9]
-        ),
-    )
-    peers(
-        "rep",
-        mine,
-        nr,
-        lambda peer: push("rep", peer, s.sm, s.sm1.at[mine], s.send_sems.at[10], s.recv_sems.at[10]),
-    )
-    pltpu.make_async_copy(part(s.gb, mine, rep_rows), s.rb.at[mine], s.recv_sems.at[9]).start()
-    pltpu.make_async_copy(s.sm, s.sm1.at[mine], s.recv_sems.at[10]).start()
-    arrived(s.sm1, s.recv_sems.at[10])
-    s.sms[...] = functools.reduce(jnp.add, [s.sm1[i] for i in range(nr)])
-    peers(
-        "dom",
-        me,
-        nd,
-        lambda peer: push("dom", peer, s.sms, s.sm2.at[me], s.send_sems.at[11], s.recv_sems.at[11]),
-    )
-    pltpu.make_async_copy(s.sms, s.sm2.at[me], s.recv_sems.at[11]).start()
-    arrived(s.rb, s.recv_sems.at[9])
-    s.gd[...] = functools.reduce(jnp.add, [s.rb[i].astype(F32) for i in range(nr)]).astype(BF16)
-    peers(
-        "dom",
-        me,
-        nd,
-        lambda peer: push(
-            "dom", peer, part(s.gd, peer, dom_rows), s.rd.at[me], s.send_sems.at[12], s.recv_sems.at[12]
-        ),
-    )
-    pltpu.make_async_copy(part(s.gd, me, dom_rows), s.rd.at[me], s.recv_sems.at[12]).start()
-    arrived(s.rd, s.recv_sems.at[12])
-    s.fin[...] = functools.reduce(jnp.add, [s.rd[i].astype(F32) for i in range(nd)]).astype(BF16)
-    place_mine = s.ag.at[mine, me]
-    peers(
-        "dom",
-        me,
-        nd,
-        lambda peer: push("dom", peer, s.fin, place_mine, s.send_sems.at[13], s.recv_sems.at[13]),
-    )
-    pltpu.make_async_copy(s.fin, place_mine, s.recv_sems.at[13]).start()
-    arrived(s.ag.at[mine], s.recv_sems.at[13])
-    peers(
-        "rep",
-        mine,
-        nr,
-        lambda peer: push(
-            "rep", peer, s.ag.at[mine], s.ag.at[mine], s.send_sems.at[14], s.recv_sems.at[14]
-        ),
-    )
-    arrived(s.sm2, s.recv_sems.at[11])
-    gsmall[...] = functools.reduce(jnp.add, [s.sm2[i] for i in range(nd)])
-    arrived(s.ag.at[pl.ds(0, nr - 1)], s.recv_sems.at[14])
-    gbig[...] = s.ag[...].reshape(rows_all, LANES)
-
-    arrived(s.fsend.at[pl.ds(0, nd - 1)], s.send_sems.at[0])
-    for first, ref in ((1, s.hsend), (3, s.zsend), (5, s.ysend), (7, s.gsend)):
-        for b in range(mb):
-            arrived(ref.at[b, pl.ds(0, nd - 1)], s.send_sems.at[first + b])
-    arrived(s.rb.at[pl.ds(0, nr - 1)], s.send_sems.at[9])
-    arrived(s.sm1.at[pl.ds(0, nr - 1)], s.send_sems.at[10])
-    arrived(s.sm2.at[pl.ds(0, nd - 1)], s.send_sems.at[11])
-    arrived(s.rd.at[pl.ds(0, nd - 1)], s.send_sems.at[12])
-    arrived(s.rd.at[pl.ds(0, nd - 1)], s.send_sems.at[13])
-    arrived(s.ag.at[pl.ds(0, nr - 1)], s.send_sems.at[14])
+        if final:
+            if split_sum:
+                sum_rep(0)
+            vector_sum(4)
+            s.sm[10:11, :head] = jnp.sum(s.accb[...].T, axis=0, keepdims=True)
+        norm_back(b)
+        if final and split_sum:
+            sum_rep(1)
+            for j in (1, 2, 3):
+                vector_sum(j)
+            attend_back(0, b, 0, middle)
+            sum_dom(0)
+            attend_back(0, b, middle)
+        else:
+            if final:
+                for j in (1, 2, 3):
+                    vector_sum(j)
+            attend_back(0, b)
+        weights_one(b)
+    vector_sum(0)
+    small_rep()
+    sum_rep(chunks - 1)
+    loaded(*range(12, 22))
+    if split_sum:
+        sum_dom(1)
+        share_dom(0)
+        small_dom()
+        sum_dom(2)
+        share_dom(1)
+        share_rep(0)
+        share_dom(2)
+        share_rep(1)
+        small_update()
+        chunk_update(0)
+        share_rep(2)
+        chunk_update(1)
+        chunk_update(2)
+    else:
+        small_dom()
+        for chunk in range(chunks):
+            sum_dom(chunk)
+        for chunk in range(chunks):
+            share_dom(chunk)
+        for chunk in range(chunks):
+            share_rep(chunk)
+        small_update()
+        for chunk in range(chunks):
+            chunk_update(chunk)
+    finish()
 
 
 def adamw(param, grad, first, second):
@@ -497,48 +605,23 @@
     )
 
 
-def adamw_kernel(hid, head, gbig, gsmall, *refs):
-    params, firsts, seconds, outs = refs[:5], refs[5:10], refs[10:15], refs[15:]
-    loss, count = outs[:2]
-    outs = outs[2:]
-    loss[...] = gsmall[12:13, 0:1]
-    total = gsmall[13:14, 0:1]
-    count[...] = total
-    scale = 1.0 / total
-
-    def update(index, grad, rows=slice(None), cols=slice(None)):
-        made = adamw(
-            params[index][rows, cols], grad, firsts[index][rows, cols], seconds[index][rows, cols]
-        )
-        for offset in range(3):
-            outs[3 * index + offset][rows, cols] = made[offset]
-
-    in_one, in_two = 3 * hid, 2 * hid + head
-    for c in range(in_one // LANES):
-        cols = slice(c * LANES, (c + 1) * LANES)
-        update(0, gbig[cols, :].astype(F32).T * scale, slice(None), cols)
-    for r in range(hid // LANES):
-        rows = slice(r * LANES, (r + 1) * LANES)
-        for c in range(0, in_two, LANES):
-            width = min(LANES, in_two - c)
-            start = in_one + r * in_two + c
-            update(
-                1, gbig[start : start + width, :].astype(F32).T * scale, rows, slice(c, c + width)
-            )
-    last = in_one + (hid // LANES) * in_two
-    update(2, gbig[last : last + head, :].astype(F32)[:, :head] * scale)
-    for j in range(5):
-        for p in range(hid // LANES):
-            row = (hid // LANES) * j + p
-            update(
-                3, gsmall[row : row + 1, :] * scale, slice(j, j + 1), slice(p * LANES, (p + 1) * LANES)
-            )
-    for j in range(2):
-        update(4, gsmall[10 + j : 11 + j, :head] * scale, slice(j, j + 1))
+def write_kernel(*refs):
+    small, held, outs = refs[0], refs[1:16], refs[16:33]
+    loss, count, sems = refs[33:]
+    loss[...] = small[12:13, 0:1]
+    count[...] = small[13:14, 0:1]
+    copies = [
+        pltpu.make_async_copy(src, dst, sems.at[i])
+        for i, (src, dst) in enumerate(zip((loss, count) + held, outs))
+    ]
+    for copy in copies:
+        copy.start()
+    for copy in copies:
+        copy.wait()
 
 
 def body(nd, nr, *args):
-    data, weights, firsts, seconds = args[:7], args[7:12], args[12:17], args[17:]
+    data, weights = args[:7], args[7:]
     features, edge_src, node_degree, send_rows, pair_src, pair_dst, pair_live = (
         a.reshape(a.shape[1:]) for a in data
     )
@@ -552,10 +635,21 @@
     head = weights[2].shape[0]
     in_one, in_two = 3 * hid, 2 * hid + head
     unit = nd * nr * 16
-    rows_all = -(-(in_one + 2 * in_two + head) // unit) * unit
-    dims = (nd, nr, mb, nodes, fan, hid, head, ext, halo, pairs, rows_all)
-    rep_rows = rows_all // nr
-    dom_rows = rep_rows // nd
+    early = (hid // LANES) * in_two
+    rows_all = -(-(early + in_one + head) // unit) * unit
+    bounds = (0, rows_all)
+    middle = rows_all - 2 * hid
+    if middle % unit == 0 and early >= unit and middle >= early + head + hid:
+        bounds = (0, early // unit * unit, middle, rows_all)
+    dims = (nd, nr, mb, nodes, fan, hid, head, ext, halo, pairs, bounds)
+    chunks = {}
+    for chunk in range(len(bounds) - 1):
+        size = (bounds[chunk + 1] - bounds[chunk]) // nr
+        chunks[f"rb{chunk}"] = pltpu.VMEM((nr, size, LANES), BF16)
+        chunks[f"gd{chunk}"] = pltpu.VMEM((size, LANES), BF16)
+        chunks[f"rd{chunk}"] = pltpu.VMEM((nd, size // nd, LANES), BF16)
+        chunks[f"fin{chunk}"] = pltpu.VMEM((size // nd, LANES), BF16)
+        chunks[f"ag{chunk}"] = pltpu.VMEM((nr, nd, size // nd, LANES), BF16)
     scratch = dict(
         ohs=pltpu.VMEM((mb, halo, nodes), BF16),
         fext=pltpu.VMEM((mb, ext, width), BF16),
@@ -569,8 +663,6 @@
         acc=pltpu.VMEM((5, hid, LANES), F32),
         accb=pltpu.VMEM((head, LANES), F32),
         sm=pltpu.VMEM((16, LANES), F32),
-        tmp=pltpu.VMEM((nodes, LANES), F32),
-        et=pltpu.VMEM((mb, 16, nodes), F32),
         oht=pltpu.VMEM((mb, ext, fan * nodes), BF16),
         tgt=pltpu.VMEM((2, mb, hid, nodes), F32),
         res1=pltpu.VMEM((mb, hid, nodes), F32),
@@ -608,43 +700,44 @@
         gw2=pltpu.VMEM((in_two, hid), F32),
         gwh=pltpu.VMEM((head, head), F32),
         gb=pltpu.VMEM((rows_all, LANES), BF16),
-        rb=pltpu.VMEM((nr, rep_rows, LANES), BF16),
-        gd=pltpu.VMEM((rep_rows, LANES), BF16),
-        rd=pltpu.VMEM((nd, dom_rows, LANES), BF16),
-        fin=pltpu.VMEM((dom_rows, LANES), BF16),
-        ag=pltpu.VMEM((nr, nd, dom_rows, LANES), BF16),
         sm1=pltpu.VMEM((nr, 16, LANES), F32),
         sms=pltpu.VMEM((16, LANES), F32),
         sm2=pltpu.VMEM((nd, 16, LANES), F32),
-        send_sems=pltpu.SemaphoreType.DMA((15,)),
-        recv_sems=pltpu.SemaphoreType.DMA((15,)),
+        load_sems=pltpu.SemaphoreType.DMA((22,)),
+        scale=pltpu.VMEM((8, LANES), F32),
+        send_sems=pltpu.SemaphoreType.DMA((23,)),
+        recv_sems=pltpu.SemaphoreType.DMA((23,)),
+        **chunks,
     )
+    operands = [features, edge_src.transpose(2, 0, 1), node_degree, send_rows, pair_src, pair_dst]
+    operands.append(pair_live.T)
+    operands += [w.T if i % 5 == 1 else w for i, w in enumerate(weights)]
+    scalars = (jax.ShapeDtypeStruct((1, 1), F32),) * 2
+    results = ()
+    for operand in operands[7:12]:
+        results += (jax.ShapeDtypeStruct(operand.shape, F32),) * 3
     whole = pl.BlockSpec(memory_space=pltpu.VMEM)
-    gbig, gsmall = pl.pallas_call(
+    anywhere = pl.BlockSpec(memory_space=pl.ANY)
+    made = pl.pallas_call(
         functools.partial(step_kernel, dims, tuple(scratch)),
-        out_shape=(
-            jax.ShapeDtypeStruct((rows_all, LANES), BF16),
-            jax.ShapeDtypeStruct((16, LANES), F32),
+        out_shape=(jax.ShapeDtypeStruct((16, LANES), F32),) + results,
+        in_specs=[anywhere] * 22,
+        out_specs=(whole,) * 16,
+        scratch_shapes=[pltpu.VMEM(a.shape, a.dtype) for a in operands] + list(scratch.values()),
+        compiler_params=pltpu.CompilerParams(
+            collective_id=0, has_side_effects=True, vmem_limit_bytes=44 * 1024 * 1024
         ),
-        in_specs=[whole] * 12,
-        out_specs=(whole, whole),
-        scratch_shapes=list(scratch.values()),
-        compiler_params=pltpu.CompilerParams(
-            collective_id=0, has_side_effects=True, vmem_limit_bytes=48 * 1024 * 1024
-        ),
-    )(features, edge_src, node_degree, send_rows, pair_src, pair_dst, pair_live, *weights)
-
-    shapes = [jax.ShapeDtypeStruct((1, 1), F32)] * 2
-    for weight in weights:
-        shapes += [jax.ShapeDtypeStruct(weight.shape, F32)] * 3
+    )(*(pltpu.with_memory_space_constraint(a, pltpu.HBM) for a in operands))
     made = pl.pallas_call(
-        functools.partial(adamw_kernel, hid, head),
-        out_shape=tuple(shapes),
-        in_specs=[whole] * 17,
-        out_specs=tuple([whole] * 17),
-        compiler_params=pltpu.CompilerParams(vmem_limit_bytes=32 * 1024 * 1024),
-    )(gbig, gsmall, *weights, *firsts, *seconds)
-    return (made[0].reshape(()), made[1].reshape(())) + tuple(made[2:])
+        write_kernel,
+        out_shape=scalars + results,
+        in_specs=[whole] * 16,
+        out_specs=(anywhere,) * 17,
+        scratch_shapes=[pltpu.VMEM((1, 1), F32)] * 2 + [pltpu.SemaphoreType.DMA((17,))],
+        compiler_params=pltpu.CompilerParams(vmem_limit_bytes=1024 * 1024),
+    )(*made)
+    loss, count = (a.reshape(()) for a in made[:2])
+    return (loss, count) + tuple(a.T if i // 3 == 1 else a for i, a in enumerate(made[2:]))
 
 
 def solution(mesh):

time: 92.5 us -> 66.1 us (0.71); the launches traced: 91.3 us -> 65.9 us
  local copies, waits for them, and re-layouts: 19 us -> 0 us
  Pallas kernels: 71.4 us -> 65 us
    unnamed x61 -> x0, local copies, waits for them, and re-layouts: 18.9 us -> none
    pallas_call x1, Pallas kernels: 69.7 us -> 63.2 us  [body(): pl.pallas_call(functools.partial(step_kernel, dims, tuple(scratch)), out_...]
where the time goes in v2:
time: 66.1 us; the launch traced here: 65.9 us
  Pallas kernels  65 us (98%)
  between operations  0.83 us (1%)
    pallas_call x1, Pallas kernels, body(): pl.pallas_call(functools.partial(step_kernel, dims, tuple(scratch)), out_...  63.2 us
    pallas_call x1, Pallas kernels, body(): pl.pallas_call(write_kernel, out_shape=scalars + results, in_specs=[whole...  1.8 us

profile of v2, /device:TPU:0, one launch (start us, length us, event | category | flops | bytes accessed | tf_op | source)
XLA Modules:
  0.0 65.9 jit_solution(12005605392500081525)
XLA Ops:
  0.7 63.2 %shard_map.341 = (f32[16,128]{1,0:T(8,128)S(1)}, f32[128,768]{1,0:T(8,128)S(1)}, f32[128,768]{1,0:T(8,128)S(1)}, f32[128,768]{1,0:T(8,128)S(1)}, f32[576,256]{1,...) custom-call(f32[2,256,128]{2,1,0:T(8,128)} %bitcast.20, ...), custom_call_target="tpu_custom_call" | custom-call | tf_op jit(solution)/shard_map/pallas_call | solution.py:721
  63.9 1.8 %shard_map.342 = (f32[1,1]{1,0:T(1,128)}, f32[1,1]{1,0:T(1,128)}, f32[128,768]{1,0:T(8,128)}, f32[128,768]{1,0:T(8,128)}, f32[128,768]{1,0:T(8,128)}, /*index=5*...) custom-call(f32[16,128]{1,0:T(8,128)S(1)} %get-tuple-element.50.refs, ...), custom_call_target="tpu_custom_call" | custom-call | tf_op jit(solution)/shard_map/pallas_call | solution.py:731

commit v3 on v2

--- a/solution.py
+++ b/solution.py
@@ -82,13 +82,21 @@
 
         lax.fori_loop(1, count, one, 0)
 
-    def push(axis, peer, src, dst, send_sem, recv_sem):
+    def others(send):
+        def one(step, carry):
+            at = lax.rem(me * nr + mine + step, nd * nr)
+            send({"dom": lax.div(at, nr), "rep": lax.rem(at, nr)})
+            return carry
+
+        lax.fori_loop(1, nd * nr, one, 0)
+
+    def push(there, src, dst, send_sem, recv_sem):
         pltpu.make_async_remote_copy(
             src_ref=src,
             dst_ref=dst,
             send_sem=send_sem,
             recv_sem=recv_sem,
-            device_id={axis: peer},
+            device_id=there,
             device_id_type=MESH,
         ).start()
 
@@ -120,28 +128,16 @@
             "dom",
             me,
             nd,
-            lambda peer: push("dom", peer, src.at[peer], dst.at[me], send_sem, recv_sem),
+            lambda peer: push({"dom": peer}, src.at[peer], dst.at[me], send_sem, recv_sem),
         )
         pltpu.make_async_copy(src.at[me], dst.at[me], recv_sem).start()
         incoming[number] = dst
         outgoing.append((number, src.at[pl.ds(0, nd - 1)]))
 
-    load(3, 0, 7, 8, 9, 10, 11, 1, 2, 4, 5, 6)
+    load(3, 0)
     barrier = pltpu.get_barrier_semaphore()
-    peers(
-        "dom",
-        me,
-        nd,
-        lambda peer: pl.semaphore_signal(barrier, inc=1, device_id={"dom": peer}, device_id_type=MESH),
-    )
-    peers(
-        "rep",
-        mine,
-        nr,
-        lambda peer: pl.semaphore_signal(barrier, inc=1, device_id={"rep": peer}, device_id_type=MESH),
-    )
-
-    load(*range(12, 22))
+    others(lambda there: pl.semaphore_signal(barrier, inc=1, device_id=there, device_id_type=MESH))
+    load(7, 8, 9, 10, 11, 1, 2, 4, 5, 6)
     loaded(3, 0)
     for b in range(mb):
         spread = (
@@ -157,8 +153,9 @@
         nn(s.ohs[b], s.fext[b, :nodes, :]).reshape(nd, halo // nd, LANES) for b in range(mb)
     ]
     s.fsend[...] = jnp.concatenate(parts, axis=1).astype(BF16)
-    pl.semaphore_wait(barrier, nd + nr - 2)
+    pl.semaphore_wait(barrier, nd * nr - 1)
     scatter_out(s.fsend, s.frecv, 0)
+    load(*range(12, 22))
 
     loaded(7, 8, 9, 10, 11)
     s.w1t[...] = w1[...].T.astype(BF16)
@@ -184,6 +181,7 @@
 
         lax.fori_loop(0, fan, one_hot, 0)
 
+        s.tab[b, :, :nodes] = nt(s.w1t[:hid, :], s.fext[b, :nodes, :]).astype(BF16)
         rest = nt(s.w1t[hid:, :], s.fext[b, :nodes, :])
         s.tgt[0, b] = rest[:hid]
         s.res1[b] = rest[hid:]
@@ -201,18 +199,19 @@
         s.cneg[b] = nt(from_src[:, half:], to_dst[:, half:])
 
     def place(index):
-        tile, which = lax.div(index, HEADS), lax.rem(index, HEADS)
-        return tile, which, aligned(which, head), aligned(tile, LANES)
+        tile, which = divmod(index, HEADS)
+        rows = slice(which * head, (which + 1) * head)
+        return tile, rows, slice(tile * LANES, (tile + 1) * LANES)
 
     def slot_at(k, tile):
-        return pl.ds(pl.multiple_of(k * nodes + tile * LANES, LANES), LANES)
+        return slice(k * nodes + tile * LANES, k * nodes + (tile + 1) * LANES)
 
     def attend(layer, b):
         att = 0 if layer == 0 else 4
         s.g[layer, b] = nn(s.tab[b], s.oht[b])
 
-        def one(index, carry):
-            tile, which, rows, cols = place(index)
+        for index in range(tiles * HEADS):
+            tile, rows, cols = place(index)
             target = s.tgt[layer, b, rows, cols]
             weight = s.vb[att, rows, :]
             count = degree[b : b + 1, cols]
@@ -233,15 +232,12 @@
                 s.al[layer, b, index, k : k + 1, :] = alpha
                 message = message + alpha * s.g[layer, b, rows, slot_at(k, tile)]
             s.msg[rows, cols] = message
-            return carry
-
-        lax.fori_loop(0, tiles * HEADS, one, 0)
 
     def attend_back(layer, b, first=0, last=None):
         att = 0 if layer == 0 else 4
 
-        def one(index, carry):
-            tile, which, rows, cols = place(index)
+        for index in range(first, tiles * HEADS if last is None else last):
+            tile, rows, cols = place(index)
             target = s.tgt[layer, b, rows, cols]
             weight = s.vb[att, rows, :]
             if layer == 0:
@@ -268,9 +264,6 @@
                 s.dg[rows, slot_at(k, tile)] = (alphas[k] * d_message + d_u).astype(BF16)
             s.dtgt[rows, cols] = d_target
             s.acc[att, rows, :] += d_att
-            return carry
-
-        lax.fori_loop(first, tiles * HEADS if last is None else last, one, 0)
 
     def pack_rows(value):
         blocks = value.reshape(nd, halo // nd, hid)
@@ -287,7 +280,7 @@
             .reshape(halo, LANES)
             .astype(BF16)
         )
-        s.tab[b] = nt(s.w1t[:hid, :], s.fext[b]).astype(BF16)
+        s.tab[b, :, nodes:] = nt(s.w1t[:hid, :], s.fext[b, nodes:, :]).astype(BF16)
         attend(0, b)
         for t in range(tiles):
             cols = slice(t * LANES, (t + 1) * LANES)
@@ -322,17 +315,9 @@
         rows = nt(s.ohs[b], s.h2t[b])
         s.zsend[b, :, :, :head] = rows.reshape(nd, halo // nd, head)
         scatter_out(s.zsend.at[b], s.zrecv.at[b], 3 + b)
-        s.h2r[b, :nodes, :] = s.h2[...].T.astype(BF16)
-
-    def pair_loss(b):
-        receive(3 + b)
-        s.h2r[b, nodes:, :] = s.zrecv[b].reshape(halo, LANES)[:, :head].astype(BF16)
-        z = nn(s.h2r[b], whb) + bias[1:2, :]
-        high, low = split(z)
-        left = jnp.concatenate([high[:nodes], high[:nodes], low[:nodes]], axis=1)
-        right = jnp.concatenate([high, low, high], axis=1)
-        score = nt(left, right)
-        pos, neg = s.cpos[b], s.cneg[b]
+        s.h2r[b] = s.h2[...].T.astype(BF16)
+
+    def pair_terms(score, pos, neg):
         small = jnp.exp(-jnp.abs(score))
         terms = (
             (pos + neg) * jnp.log1p(small)
@@ -343,12 +328,24 @@
         big = 1.0 / (1.0 + small)
         little = small * big
         up = score > 0.0
-        d_score = neg * jnp.where(up, big, little) - pos * jnp.where(up, little, big)
-        d_low = d_score.astype(BF16)
-        d_table = tn(d_low, high[:nodes])
-        s.dz[b] = nn(d_low, high) + d_table[:nodes]
-        s.ysend[b, :, :, :head] = d_table[nodes:].reshape(nd, halo // nd, head)
+        return (neg * jnp.where(up, big, little) - pos * jnp.where(up, little, big)).astype(BF16)
+
+    def pair_own(b):
+        high, low = split(nn(s.h2r[b], whb) + bias[1:2, :])
+        s.left[b] = jnp.concatenate([high, high, low], axis=1)
+        score = nt(s.left[b], jnp.concatenate([high, low, high], axis=1))
+        d_score = pair_terms(score, s.cpos[b, :, :nodes], s.cneg[b, :, :nodes])
+        s.dz[b] = nn(d_score, high) + tn(d_score, high)
+
+    def pair_halo(b):
+        receive(3 + b)
+        rows = s.zrecv[b].reshape(halo, LANES)[:, :head].astype(BF16)
+        high, low = split(nn(rows, whb) + bias[1:2, :])
+        score = nt(s.left[b], jnp.concatenate([high, low, high], axis=1))
+        d_score = pair_terms(score, s.cpos[b, :, nodes:], s.cneg[b, :, nodes:])
+        s.ysend[b, :, :, :head] = tn(d_score, s.left[b, :, :head]).reshape(nd, halo // nd, head)
         scatter_out(s.ysend.at[b], s.yrecv.at[b], 5 + b)
+        s.dz[b] += nn(d_score, high)
 
     def add_to(ref, value, b):
         if b == 0:
@@ -362,26 +359,28 @@
         dz = s.dz[b] + tn(s.ohs[b], returned)
         s.sm[11:12, :head] += jnp.sum(dz, axis=0, keepdims=True)
         dz_low = dz.astype(BF16)
+        d_out = nt(whb, dz_low)
+        s.dmsg[:head, :] = d_out * (1.0 / HEADS)
+        s.dproj2[b, 2 * hid :, :] = d_out.astype(BF16)
+        attend_back(1, b)
+        d_table = nt(s.dg[...], s.oht[b])
+        s.gsend[b] = pack_rows(d_table[:, nodes:].T)
+        scatter_out(s.gsend.at[b], s.grecv.at[b], 7 + b)
+        s.dsrc[b] = d_table[:, :nodes]
+        s.dproj2[b, hid : 2 * hid, :] = s.dtgt[...].astype(BF16)
+        s.dhp[b] = nn(s.w2b[:, hid:], s.dproj2[b, hid:, :])
+        add_to(s.gw2.at[hid:, :], nt(s.dproj2[b, hid:, :], s.h1t[b]), b)
         add_to(s.gwh, nn(s.h2t[b], dz_low), b)
-        d_out = nt(whb, dz_low)
-        s.dres2[b] = d_out.astype(BF16)
-        s.dmsg[:head, :] = d_out * (1.0 / HEADS)
         s.accb[...] += functools.reduce(
             jnp.add, [d_out[:, t * LANES : (t + 1) * LANES] for t in range(tiles)]
         )
-        attend_back(1, b)
-        s.dproj2[b, hid : 2 * hid, :] = s.dtgt[...].astype(BF16)
-        s.dproj2[b, 2 * hid :, :] = s.dres2[b]
-        s.gsend[b] = pack_rows(nt(s.oht[b, nodes:, :], s.dg[...]))
-        scatter_out(s.gsend.at[b], s.grecv.at[b], 7 + b)
-        s.dsrc[b] = nt(s.dg[...], s.oht[b, :nodes, :])
 
     def finish_two(b):
         receive(7 + b)
         returned = unpack_rows(s.grecv.at[b]).astype(BF16)
         s.dproj2[b, :hid, :] = (s.dsrc[b] + tn(returned, s.ohs[b])).astype(BF16)
-        add_to(s.gw2, nt(s.dproj2[b], s.h1t[b]), b)
-        s.dh[...] = nn(s.w2b[...], s.dproj2[b])
+        s.dh[...] = s.dhp[b] + nn(s.w2b[:, :hid], s.dproj2[b, :hid, :])
+        add_to(s.gw2.at[:hid, :], nt(s.dproj2[b, :hid, :], s.h1t[b]), b)
 
     def norm_back(b):
         for t in range(tiles):
@@ -415,7 +414,7 @@
             axis,
             index,
             count,
-            lambda peer: push(axis, peer, src_of(peer), dst.at[index], send_sem, recv_sem),
+            lambda peer: push({axis: peer}, src_of(peer), dst.at[index], send_sem, recv_sem),
         )
         if own:
             pltpu.make_async_copy(src_of(index), dst.at[index], recv_sem).start()
@@ -427,6 +426,7 @@
     def summed(ref, count):
         return functools.reduce(jnp.add, [ref[i].astype(F32) for i in range(count)])
 
+    chunks = len(bounds) - 1
     in_one, in_two = 3 * hid, 2 * hid + head
     regions = [(i * in_two, s.gw2, slice(None), slice(i * LANES, (i + 1) * LANES)) for i in range(hid // LANES)]
     start = (hid // LANES) * in_two
@@ -474,6 +474,29 @@
         ag = chunk_of(chunk)[4]
         receive(13 + 4 * chunk)
         exchange("rep", 14 + 4 * chunk, lambda peer: ag.at[mine], ag, own=False)
+
+    def exchange_all(number, src_of, dst):
+        index = me * nr + mine
+        send_sem, recv_sem = s.send_sems.at[number], s.recv_sems.at[number]
+        others(
+            lambda there: push(
+                there, src_of(there["dom"] * nr + there["rep"]), dst.at[index], send_sem, recv_sem
+            )
+        )
+        pltpu.make_async_copy(src_of(index), dst.at[index], recv_sem).start()
+        incoming[number] = dst
+        outgoing.append((number, dst.at[pl.ds(0, nd * nr - 1)]))
+
+    def sum_all():
+        pack(chunks - 1)
+        size = (bounds[-1] - bounds[-2]) // (nd * nr)
+        here = s.gb.at[bounds[-2] : bounds[-1], :]
+        exchange_all(19, lambda at: part(here, at, size), s.rl)
+
+    def share_all():
+        receive(19)
+        s.finl[...] = summed(s.rl, nd * nr).astype(BF16)
+        exchange_all(20, lambda at: s.finl, s.agl)
 
     def vector_sum(j):
         total = jnp.sum(s.acc[j].T, axis=0, keepdims=True)
@@ -513,8 +536,8 @@
             update(4, total[10 + j : 11 + j, :head] * scale, slice(j, j + 1), slice(None))
 
     def chunk_update(chunk):
-        ag = chunk_of(chunk)[4]
-        receive(14 + 4 * chunk)
+        ag = s.agl if chunk == chunks - 1 else chunk_of(chunk)[4]
+        receive(20 if chunk == chunks - 1 else 14 + 4 * chunk)
         low, high = bounds[chunk], bounds[chunk + 1]
         whole = ag[...].reshape(high - low, LANES)
         scale = s.scale[0:1, 0:1]
@@ -532,11 +555,10 @@
     s.gb[...] = jnp.zeros_like(s.gb)
     s.sm[13:14, 0:1] = 2.0 * jnp.sum(plive[...].astype(F32), axis=1, keepdims=True)
     receive(0)
-    stages = [(stage, b) for stage in (layer_one, layer_two, pair_loss, back_two) for b in range(mb)]
+    stages = [(stage, b) for stage in (layer_one, layer_two, pair_own, pair_halo, back_two) for b in range(mb)]
     for stage, b in stages:
         stage(b)
 
-    chunks = len(bounds) - 1
     split_sum = chunks == 3
     middle = tiles * HEADS // 2
     for b in range(mb):
@@ -561,35 +583,24 @@
                     vector_sum(j)
             attend_back(0, b)
         weights_one(b)
+    sum_all()
     vector_sum(0)
     small_rep()
-    sum_rep(chunks - 1)
     loaded(*range(12, 22))
     if split_sum:
         sum_dom(1)
         share_dom(0)
         small_dom()
-        sum_dom(2)
         share_dom(1)
-        share_rep(0)
-        share_dom(2)
-        share_rep(1)
-        small_update()
-        chunk_update(0)
-        share_rep(2)
-        chunk_update(1)
-        chunk_update(2)
     else:
         small_dom()
-        for chunk in range(chunks):
-            sum_dom(chunk)
-        for chunk in range(chunks):
-            share_dom(chunk)
-        for chunk in range(chunks):
-            share_rep(chunk)
-        small_update()
-        for chunk in range(chunks):
-            chunk_update(chunk)
+    share_all()
+    if split_sum:
+        share_rep(0)
+        share_rep(1)
+    small_update()
+    for chunk in range(chunks):
+        chunk_update(chunk)
     finish()
 
 
@@ -643,7 +654,11 @@
         bounds = (0, early // unit * unit, middle, rows_all)
     dims = (nd, nr, mb, nodes, fan, hid, head, ext, halo, pairs, bounds)
     chunks = {}
-    for chunk in range(len(bounds) - 1):
+    last = bounds[-1] - bounds[-2]
+    for name in ("rl", "agl"):
+        chunks[name] = pltpu.VMEM((nd * nr, last // (nd * nr), LANES), BF16)
+    chunks["finl"] = pltpu.VMEM((last // (nd * nr), LANES), BF16)
+    for chunk in range(len(bounds) - 2):
         size = (bounds[chunk + 1] - bounds[chunk]) // nr
         chunks[f"rb{chunk}"] = pltpu.VMEM((nr, size, LANES), BF16)
         chunks[f"gd{chunk}"] = pltpu.VMEM((size, LANES), BF16)
@@ -681,14 +696,15 @@
         own2=pltpu.VMEM((mb, hid, nodes), BF16),
         h2=pltpu.VMEM((head, nodes), F32),
         h2t=pltpu.VMEM((mb, head, nodes), BF16),
-        h2r=pltpu.VMEM((mb, ext, head), BF16),
+        h2r=pltpu.VMEM((mb, nodes, head), BF16),
+        left=pltpu.VMEM((mb, nodes, 3 * head), BF16),
+        dhp=pltpu.VMEM((mb, hid, nodes), F32),
         zsend=pltpu.VMEM((mb, nd, per, LANES), F32),
         zrecv=pltpu.VMEM((mb, nd, per, LANES), F32),
         ysend=pltpu.VMEM((mb, nd, per, LANES), F32),
         yrecv=pltpu.VMEM((mb, nd, per, LANES), F32),
         dz=pltpu.VMEM((mb, nodes, head), F32),
         dmsg=pltpu.VMEM((hid, nodes), F32),
-        dres2=pltpu.VMEM((mb, head, nodes), BF16),
         dtgt=pltpu.VMEM((hid, nodes), F32),
         dg=pltpu.VMEM((hid, fan * nodes), BF16),
         dproj2=pltpu.VMEM((mb, in_two, nodes), BF16),
@@ -705,8 +721,8 @@
         sm2=pltpu.VMEM((nd, 16, LANES), F32),
         load_sems=pltpu.SemaphoreType.DMA((22,)),
         scale=pltpu.VMEM((8, LANES), F32),
-        send_sems=pltpu.SemaphoreType.DMA((23,)),
-        recv_sems=pltpu.SemaphoreType.DMA((23,)),
+        send_sems=pltpu.SemaphoreType.DMA((21,)),
+        recv_sems=pltpu.SemaphoreType.DMA((21,)),
         **chunks,
     )
     operands = [features, edge_src.transpose(2, 0, 1), node_degree, send_rows, pair_src, pair_dst]

time: 66.1 us -> 60.4 us (0.914)
  Pallas kernels: 65 us -> 59.3 us
    pallas_call x1, Pallas kernels: 63.2 us -> 57.5 us  [body(): pl.pallas_call(functools.partial(step_kernel, dims, tuple(scratch)), out_...]
where the time goes in v3:
time: 60.4 us; the launch traced here: 60.2 us
  Pallas kernels  59.3 us (98%)
  between operations  0.83 us (1%)
    pallas_call x1, Pallas kernels, body(): pl.pallas_call(functools.partial(step_kernel, dims, tuple(scratch)), out_...  57.5 us
    pallas_call x1, Pallas kernels, body(): pl.pallas_call(write_kernel, out_shape=scalars + results, in_specs=[whole...  1.8 us

profile of v3, /device:TPU:0, one launch (start us, length us, event | category | flops | bytes accessed | tf_op | source)
XLA Modules:
  0.0 60.2 jit_solution(4169533458835557483)
XLA Ops:
  0.7 57.5 %shard_map.341 = (f32[16,128]{1,0:T(8,128)S(1)}, f32[128,768]{1,0:T(8,128)S(1)}, f32[128,768]{1,0:T(8,128)S(1)}, f32[128,768]{1,0:T(8,128)S(1)}, f32[576,256]{1,...) custom-call(f32[2,256,128]{2,1,0:T(8,128)} %bitcast.20, ...), custom_call_target="tpu_custom_call" | custom-call | tf_op jit(solution)/shard_map/pallas_call | solution.py:737
  58.2 1.8 %shard_map.342 = (f32[1,1]{1,0:T(1,128)}, f32[1,1]{1,0:T(1,128)}, f32[128,768]{1,0:T(8,128)}, f32[128,768]{1,0:T(8,128)}, f32[128,768]{1,0:T(8,128)}, /*index=5*...) custom-call(f32[16,128]{1,0:T(8,128)S(1)} %get-tuple-element.50.refs, ...), custom_call_target="tpu_custom_call" | custom-call | tf_op jit(solution)/shard_map/pallas_call | solution.py:747

commit v4 on v3

--- a/solution.py
+++ b/solution.py
@@ -138,7 +138,7 @@
     barrier = pltpu.get_barrier_semaphore()
     others(lambda there: pl.semaphore_signal(barrier, inc=1, device_id=there, device_id_type=MESH))
     load(7, 8, 9, 10, 11, 1, 2, 4, 5, 6)
-    loaded(3, 0)
+    loaded(3)
     for b in range(mb):
         spread = (
             lax.div(row_iota(halo, nd), halo // nd) == lane_iota(halo, nd)
@@ -147,8 +147,10 @@
         pick = lax.rem(row_iota(halo, halo // nd), halo // nd) == lane_iota(halo, halo // nd)
         column = jnp.sum(jnp.where(pick, listed, 0.0), axis=1, keepdims=True)
         s.ohs[b] = (lane_iota(halo, nodes).astype(F32) == column).astype(F32).astype(BF16)
+
+    loaded(0)
+    for b in range(mb):
         s.fext[b, :nodes, :] = feats[b].astype(BF16)
-
     parts = [
         nn(s.ohs[b], s.fext[b, :nodes, :]).reshape(nd, halo // nd, LANES) for b in range(mb)
     ]
@@ -233,13 +235,11 @@
                 message = message + alpha * s.g[layer, b, rows, slot_at(k, tile)]
             s.msg[rows, cols] = message
 
-    def attend_back(layer, b, first=0, last=None):
+    def attend_back(layer, b):
         att = 0 if layer == 0 else 4
 
-        for index in range(first, tiles * HEADS if last is None else last):
+        for index in range(tiles * HEADS):
             tile, rows, cols = place(index)
-            target = s.tgt[layer, b, rows, cols]
-            weight = s.vb[att, rows, :]
             if layer == 0:
                 d_message = s.dmsg[rows, cols]
             else:
@@ -254,16 +254,26 @@
             d_att = jnp.zeros((head, LANES), F32)
             for k in range(fan):
                 d_score = alphas[k] * (d_alphas[k] - total)
+                d_u = d_score * s.slope[layer, b, rows, slot_at(k, tile)].astype(F32)
+                d_target = d_target + d_u
+                d_att = d_att + d_score * s.mixed[layer, b, rows, slot_at(k, tile)].astype(F32)
+                s.dg[rows, slot_at(k, tile)] = (alphas[k] * d_message + d_u).astype(BF16)
+            s.dtgt[rows, cols] = d_target
+            s.acc[att, rows, :] += d_att
+
+    def slopes(layer, b):
+        att = 0 if layer == 0 else 4
+        for index in range(tiles * HEADS):
+            tile, rows, cols = place(index)
+            target = s.tgt[layer, b, rows, cols]
+            weight = s.vb[att, rows, :]
+            for k in range(fan):
                 u = s.g[layer, b, rows, slot_at(k, tile)] + target
                 gate = sigmoid(u)
                 mixed = u * gate
-                slope = gate * (1.0 + (u - mixed))
-                d_u = (d_score * weight) * slope
-                d_target = d_target + d_u
-                d_att = d_att + d_score * mixed
-                s.dg[rows, slot_at(k, tile)] = (alphas[k] * d_message + d_u).astype(BF16)
-            s.dtgt[rows, cols] = d_target
-            s.acc[att, rows, :] += d_att
+                s.mixed[layer, b, rows, slot_at(k, tile)] = mixed.astype(BF16)
+                slope = weight * (gate * (1.0 + (u - mixed)))
+                s.slope[layer, b, rows, slot_at(k, tile)] = slope.astype(BF16)
 
     def pack_rows(value):
         blocks = value.reshape(nd, halo // nd, hid)
@@ -303,7 +313,8 @@
     def layer_two(b):
         receive(1 + b)
         s.tab[b, :, :nodes] = s.own2[b]
-        s.tab[b, :, nodes:] = nt(s.w2t[:hid, :], unpack_rows(s.hrecv.at[b]).astype(BF16)).astype(BF16)
+        s.h1h[b] = unpack_rows(s.hrecv.at[b]).astype(BF16)
+        s.tab[b, :, nodes:] = nt(s.w2t[:hid, :], s.h1h[b]).astype(BF16)
         attend(1, b)
         for t in range(tiles):
             cols = slice(t * LANES, (t + 1) * LANES)
@@ -366,21 +377,26 @@
         d_table = nt(s.dg[...], s.oht[b])
         s.gsend[b] = pack_rows(d_table[:, nodes:].T)
         scatter_out(s.gsend.at[b], s.grecv.at[b], 7 + b)
-        s.dsrc[b] = d_table[:, :nodes]
-        s.dproj2[b, hid : 2 * hid, :] = s.dtgt[...].astype(BF16)
-        s.dhp[b] = nn(s.w2b[:, hid:], s.dproj2[b, hid:, :])
-        add_to(s.gw2.at[hid:, :], nt(s.dproj2[b, hid:, :], s.h1t[b]), b)
-        add_to(s.gwh, nn(s.h2t[b], dz_low), b)
+        s.dtab[b] = d_table
+        s.dzl[b] = dz_low
         s.accb[...] += functools.reduce(
             jnp.add, [d_out[:, t * LANES : (t + 1) * LANES] for t in range(tiles)]
         )
+        s.dproj2[b, hid : 2 * hid, :] = s.dtgt[...].astype(BF16)
+
+    def after_two(b):
+        s.dhp[b] = nn(s.w2b[:, hid:], s.dproj2[b, hid:, :])
+        add_to(s.gw2.at[hid:, :], nt(s.dproj2[b, hid:, :], s.h1t[b]), b)
+        d_own = s.dtab[b, :, :nodes].astype(BF16)
+        d_halo = s.dtab[b, :, nodes:].astype(BF16)
+        add_to(s.gw2.at[:hid, :], nt(d_own, s.h1t[b]) + nn(d_halo, s.h1h[b]), b)
+        add_to(s.gwh, nn(s.h2t[b], s.dzl[b]), b)
 
     def finish_two(b):
         receive(7 + b)
         returned = unpack_rows(s.grecv.at[b]).astype(BF16)
-        s.dproj2[b, :hid, :] = (s.dsrc[b] + tn(returned, s.ohs[b])).astype(BF16)
-        s.dh[...] = s.dhp[b] + nn(s.w2b[:, :hid], s.dproj2[b, :hid, :])
-        add_to(s.gw2.at[:hid, :], nt(s.dproj2[b, :hid, :], s.h1t[b]), b)
+        d_source = s.dtab[b, :, :nodes] + tn(returned, s.ohs[b])
+        s.dh[...] = s.dhp[b] + nn(s.w2b[:, :hid], d_source.astype(BF16))
 
     def norm_back(b):
         for t in range(tiles):
@@ -396,6 +412,8 @@
             dy = s.rstd[b, 0:1, cols] * (dx - mean - normed * along)
             s.acc[1] += dy
             s.dmsg[:, cols] = dy
+
+    def resid_one(b):
         add_to(s.gw1.at[2 * hid :, :], nn(s.dmsg[...].astype(BF16), s.fext[b, :nodes, :]), b)
 
     def weights_one(b):
@@ -427,11 +445,16 @@
         return functools.reduce(jnp.add, [ref[i].astype(F32) for i in range(count)])
 
     chunks = len(bounds) - 1
+    split_sum = chunks == 3
     in_one, in_two = 3 * hid, 2 * hid + head
-    regions = [(i * in_two, s.gw2, slice(None), slice(i * LANES, (i + 1) * LANES)) for i in range(hid // LANES)]
-    start = (hid // LANES) * in_two
-    regions.append((start, s.gwh, slice(None), slice(None)))
-    regions.append((start + head, s.gw1, slice(2 * hid, None), slice(None)))
+    halves = [slice(i * LANES, (i + 1) * LANES) for i in range(hid // LANES)]
+    regions, start = [], 0
+    for rows in (slice(hid, 2 * hid), slice(0, hid), slice(2 * hid, in_two)):
+        for cols in halves:
+            regions.append((start, s.gw2, rows, cols))
+            start += rows.stop - rows.start
+    regions.append((start, s.gwh, slice(0, head), slice(None)))
+    regions.append((start + head, s.gw1, slice(2 * hid, in_one), slice(None)))
     regions.append((bounds[-1] - 2 * hid, s.gw1, slice(0, 2 * hid), slice(None)))
 
     def spans(chunk):
@@ -487,16 +510,21 @@
         incoming[number] = dst
         outgoing.append((number, dst.at[pl.ds(0, nd * nr - 1)]))
 
-    def sum_all():
-        pack(chunks - 1)
-        size = (bounds[-1] - bounds[-2]) // (nd * nr)
-        here = s.gb.at[bounds[-2] : bounds[-1], :]
-        exchange_all(19, lambda at: part(here, at, size), s.rl)
-
-    def share_all():
-        receive(19)
-        s.finl[...] = summed(s.rl, nd * nr).astype(BF16)
-        exchange_all(20, lambda at: s.finl, s.agl)
+    def direct(chunk):
+        return [getattr(s, f"{name}{chunk}") for name in ("rl", "finl", "agl")]
+
+    def sum_all(chunk):
+        pack(chunk)
+        rl, finl, agl = direct(chunk)
+        size = finl.shape[0]
+        here = s.gb.at[bounds[chunk] : bounds[chunk + 1], :]
+        exchange_all(11 + 4 * chunk, lambda at: part(here, at, size), rl)
+
+    def share_all(chunk):
+        rl, finl, agl = direct(chunk)
+        receive(11 + 4 * chunk)
+        finl[...] = summed(rl, nd * nr).astype(BF16)
+        exchange_all(12 + 4 * chunk, lambda at: finl, agl)
 
     def vector_sum(j):
         total = jnp.sum(s.acc[j].T, axis=0, keepdims=True)
@@ -536,8 +564,9 @@
             update(4, total[10 + j : 11 + j, :head] * scale, slice(j, j + 1), slice(None))
 
     def chunk_update(chunk):
-        ag = s.agl if chunk == chunks - 1 else chunk_of(chunk)[4]
-        receive(20 if chunk == chunks - 1 else 14 + 4 * chunk)
+        staged_sum = split_sum and chunk < 2
+        ag = chunk_of(chunk)[4] if staged_sum else direct(chunk)[2]
+        receive(4 * chunk + (14 if staged_sum else 12))
         low, high = bounds[chunk], bounds[chunk + 1]
         whole = ag[...].reshape(high - low, LANES)
         scale = s.scale[0:1, 0:1]
@@ -555,48 +584,48 @@
     s.gb[...] = jnp.zeros_like(s.gb)
     s.sm[13:14, 0:1] = 2.0 * jnp.sum(plive[...].astype(F32), axis=1, keepdims=True)
     receive(0)
-    stages = [(stage, b) for stage in (layer_one, layer_two, pair_own, pair_halo, back_two) for b in range(mb)]
+    stages = [(stage, b) for stage in (layer_one, layer_two, pair_own) for b in range(mb)]
+    for b in range(mb):
+        stages += [(pair_halo, b), (functools.partial(slopes, 1), b)]
+    stages += [(functools.partial(slopes, 0), 0)]
+    stages += [(back_two, b) for b in range(mb)]
     for stage, b in stages:
         stage(b)
 
-    split_sum = chunks == 3
-    middle = tiles * HEADS // 2
     for b in range(mb):
-        final = b == mb - 1
+        after_two(b)
+    if split_sum:
+        sum_rep(0)
+    for b in range(1, mb):
+        slopes(0, b)
+    vector_sum(4)
+    s.sm[10:11, :head] = jnp.sum(s.accb[...].T, axis=0, keepdims=True)
+    for b in range(mb):
+        final = split_sum and b == mb - 1
         finish_two(b)
+        norm_back(b)
+        resid_one(b)
         if final:
-            if split_sum:
-                sum_rep(0)
-            vector_sum(4)
-            s.sm[10:11, :head] = jnp.sum(s.accb[...].T, axis=0, keepdims=True)
-        norm_back(b)
-        if final and split_sum:
             sum_rep(1)
-            for j in (1, 2, 3):
-                vector_sum(j)
-            attend_back(0, b, 0, middle)
+        attend_back(0, b)
+        weights_one(b)
+        if split_sum and b == mb - 2:
             sum_dom(0)
-            attend_back(0, b, middle)
-        else:
-            if final:
-                for j in (1, 2, 3):
-                    vector_sum(j)
-            attend_back(0, b)
-        weights_one(b)
-    sum_all()
-    vector_sum(0)
+    sum_all(chunks - 1)
+    if split_sum:
+        sum_dom(1)
+        share_dom(0)
+    for j in range(4):
+        vector_sum(j)
     small_rep()
     loaded(*range(12, 22))
     if split_sum:
-        sum_dom(1)
-        share_dom(0)
-        small_dom()
         share_dom(1)
-    else:
-        small_dom()
-    share_all()
+    share_all(chunks - 1)
+    small_dom()
     if split_sum:
         share_rep(0)
+    if split_sum:
         share_rep(1)
     small_update()
     for chunk in range(chunks):
@@ -646,25 +675,28 @@
     head = weights[2].shape[0]
     in_one, in_two = 3 * hid, 2 * hid + head
     unit = nd * nr * 16
-    early = (hid // LANES) * in_two
-    rows_all = -(-(early + in_one + head) // unit) * unit
+    quarter = (hid // LANES) * hid
+    used = 2 * quarter + (hid // LANES + 1) * head + in_one
+    rows_all = -(-used // unit) * unit
     bounds = (0, rows_all)
-    middle = rows_all - 2 * hid
-    if middle % unit == 0 and early >= unit and middle >= early + head + hid:
-        bounds = (0, early // unit * unit, middle, rows_all)
+    if quarter % unit == 0 and 2 * hid % unit == 0:
+        bounds = (0, 2 * quarter, rows_all - 2 * hid, rows_all)
     dims = (nd, nr, mb, nodes, fan, hid, head, ext, halo, pairs, bounds)
     chunks = {}
-    last = bounds[-1] - bounds[-2]
-    for name in ("rl", "agl"):
-        chunks[name] = pltpu.VMEM((nd * nr, last // (nd * nr), LANES), BF16)
-    chunks["finl"] = pltpu.VMEM((last // (nd * nr), LANES), BF16)
-    for chunk in range(len(bounds) - 2):
-        size = (bounds[chunk + 1] - bounds[chunk]) // nr
-        chunks[f"rb{chunk}"] = pltpu.VMEM((nr, size, LANES), BF16)
-        chunks[f"gd{chunk}"] = pltpu.VMEM((size, LANES), BF16)
-        chunks[f"rd{chunk}"] = pltpu.VMEM((nd, size // nd, LANES), BF16)
-        chunks[f"fin{chunk}"] = pltpu.VMEM((size // nd, LANES), BF16)
-        chunks[f"ag{chunk}"] = pltpu.VMEM((nr, nd, size // nd, LANES), BF16)
+    for chunk in range(len(bounds) - 1):
+        rows = bounds[chunk + 1] - bounds[chunk]
+        if len(bounds) > 2 and chunk < 2:
+            size = rows // nr
+            chunks[f"rb{chunk}"] = pltpu.VMEM((nr, size, LANES), BF16)
+            chunks[f"gd{chunk}"] = pltpu.VMEM((size, LANES), BF16)
+            chunks[f"rd{chunk}"] = pltpu.VMEM((nd, size // nd, LANES), BF16)
+            chunks[f"fin{chunk}"] = pltpu.VMEM((size // nd, LANES), BF16)
+            chunks[f"ag{chunk}"] = pltpu.VMEM((nr, nd, size // nd, LANES), BF16)
+        else:
+            size = rows // (nd * nr)
+            chunks[f"rl{chunk}"] = pltpu.VMEM((nd * nr, size, LANES), BF16)
+            chunks[f"finl{chunk}"] = pltpu.VMEM((size, LANES), BF16)
+            chunks[f"agl{chunk}"] = pltpu.VMEM((nd * nr, size, LANES), BF16)
     scratch = dict(
         ohs=pltpu.VMEM((mb, halo, nodes), BF16),
         fext=pltpu.VMEM((mb, ext, width), BF16),
@@ -686,6 +718,8 @@
         cneg=pltpu.VMEM((mb, nodes, ext), F32),
         tab=pltpu.VMEM((mb, hid, ext), BF16),
         g=pltpu.VMEM((2, mb, hid, fan * nodes), F32),
+        mixed=pltpu.VMEM((2, mb, hid, fan * nodes), BF16),
+        slope=pltpu.VMEM((2, mb, hid, fan * nodes), BF16),
         al=pltpu.VMEM((2, mb, (nodes // LANES) * HEADS, 16, LANES), F32),
         msg=pltpu.VMEM((hid, nodes), F32),
         xhat=pltpu.VMEM((mb, hid, nodes), F32),
@@ -699,6 +733,7 @@
         h2r=pltpu.VMEM((mb, nodes, head), BF16),
         left=pltpu.VMEM((mb, nodes, 3 * head), BF16),
         dhp=pltpu.VMEM((mb, hid, nodes), F32),
+        dzl=pltpu.VMEM((mb, nodes, head), BF16),
         zsend=pltpu.VMEM((mb, nd, per, LANES), F32),
         zrecv=pltpu.VMEM((mb, nd, per, LANES), F32),
         ysend=pltpu.VMEM((mb, nd, per, LANES), F32),
@@ -708,7 +743,8 @@
         dtgt=pltpu.VMEM((hid, nodes), F32),
         dg=pltpu.VMEM((hid, fan * nodes), BF16),
         dproj2=pltpu.VMEM((mb, in_two, nodes), BF16),
-        dsrc=pltpu.VMEM((mb, hid, nodes), F32),
+        dtab=pltpu.VMEM((mb, hid, ext), F32),
+        h1h=pltpu.VMEM((mb, halo, hid), BF16),
         gsend=pltpu.VMEM((mb, nd, 2 * per, LANES), BF16),
         grecv=pltpu.VMEM((mb, nd, 2 * per, LANES), BF16),
         dh=pltpu.VMEM((hid, nodes), F32),
@@ -721,8 +757,8 @@
         sm2=pltpu.VMEM((nd, 16, LANES), F32),
         load_sems=pltpu.SemaphoreType.DMA((22,)),
         scale=pltpu.VMEM((8, LANES), F32),
-        send_sems=pltpu.SemaphoreType.DMA((21,)),
-        recv_sems=pltpu.SemaphoreType.DMA((21,)),
+        send_sems=pltpu.SemaphoreType.DMA((27,)),
+        recv_sems=pltpu.SemaphoreType.DMA((27,)),
         **chunks,
     )
     operands = [features, edge_src.transpose(2, 0, 1), node_degree, send_rows, pair_src, pair_dst]
@@ -741,7 +777,7 @@
         out_specs=(whole,) * 16,
         scratch_shapes=[pltpu.VMEM(a.shape, a.dtype) for a in operands] + list(scratch.values()),
         compiler_params=pltpu.CompilerParams(
-            collective_id=0, has_side_effects=True, vmem_limit_bytes=44 * 1024 * 1024
+            collective_id=0, has_side_effects=True, vmem_limit_bytes=(34 + ext // 32) * 1024 * 1024
         ),
     )(*(pltpu.with_memory_space_constraint(a, pltpu.HBM) for a in operands))
     made = pl.pallas_call(

time: 60.4 us -> 55.3 us (0.916)
  Pallas kernels: 59.3 us -> 54.3 us
    pallas_call x1, Pallas kernels: 57.5 us -> 52.5 us  [body(): pl.pallas_call(functools.partial(step_kernel, dims, tuple(scratch)), out_...]
where the time goes in v4:
time: 55.3 us; the launch traced here: 55.1 us
  Pallas kernels  54.3 us (98%)
  between operations  0.83 us (2%)
    pallas_call x1, Pallas kernels, body(): pl.pallas_call(functools.partial(step_kernel, dims, tuple(scratch)), out_...  52.5 us
    pallas_call x1, Pallas kernels, body(): pl.pallas_call(write_kernel, out_shape=scalars + results, in_specs=[whole...  1.8 us

profile of v4, /device:TPU:0, one launch (start us, length us, event | category | flops | bytes accessed | tf_op | source)
XLA Modules:
  0.0 55.1 jit_solution(10582814858472223370)
XLA Ops:
  0.7 52.5 %shard_map.341 = (f32[16,128]{1,0:T(8,128)S(1)}, f32[128,768]{1,0:T(8,128)S(1)}, f32[128,768]{1,0:T(8,128)S(1)}, f32[128,768]{1,0:T(8,128)S(1)}, f32[576,256]{1,...) custom-call(f32[2,256,128]{2,1,0:T(8,128)} %bitcast.20, ...), custom_call_target="tpu_custom_call" | custom-call | tf_op jit(solution)/shard_map/pallas_call | solution.py:773
  53.2 1.8 %shard_map.342 = (f32[1,1]{1,0:T(1,128)}, f32[1,1]{1,0:T(1,128)}, f32[128,768]{1,0:T(8,128)}, f32[128,768]{1,0:T(8,128)}, f32[128,768]{1,0:T(8,128)}, /*index=5*...) custom-call(f32[16,128]{1,0:T(8,128)S(1)} %get-tuple-element.50.refs, ...), custom_call_target="tpu_custom_call" | custom-call | tf_op jit(solution)/shard_map/pallas_call | solution.py:783

commit v5 on v4

--- a/solution.py
+++ b/solution.py
@@ -160,6 +160,8 @@
     load(*range(12, 22))
 
     loaded(7, 8, 9, 10, 11)
+    for b in range(mb):
+        s.ohst[b] = s.ohs[b].astype(F32).T.astype(BF16)
     s.w1t[...] = w1[...].T.astype(BF16)
     s.w2t[...] = w2[...].astype(BF16)
     s.w2b[...] = w2[...].T.astype(BF16)
@@ -305,6 +307,8 @@
             s.h1t[b, :, cols] = jnp.where(n > 0.0, n, jnp.exp(jnp.minimum(n, 0.0)) - 1.0).astype(BF16)
         s.hsend[b] = pack_rows(nt(s.ohs[b], s.h1t[b]))
         scatter_out(s.hsend.at[b], s.hrecv.at[b], 1 + b)
+
+    def project_two(b):
         own = nn(s.w2t[...], s.h1t[b])
         s.own2[b] = own[:hid].astype(BF16)
         s.tgt[1, b] = own[hid : 2 * hid]
@@ -335,17 +339,19 @@
             + pos * jnp.maximum(-score, 0.0)
             + neg * jnp.maximum(score, 0.0)
         )
-        s.sm[12:13, 0:1] += jnp.sum(jnp.sum(terms, axis=0, keepdims=True), axis=1, keepdims=True)
+        total = jnp.sum(jnp.sum(terms, axis=0, keepdims=True), axis=1, keepdims=True)
         big = 1.0 / (1.0 + small)
         little = small * big
         up = score > 0.0
-        return (neg * jnp.where(up, big, little) - pos * jnp.where(up, little, big)).astype(BF16)
+        d_score = neg * jnp.where(up, big, little) - pos * jnp.where(up, little, big)
+        return d_score.astype(BF16), total
 
     def pair_own(b):
         high, low = split(nn(s.h2r[b], whb) + bias[1:2, :])
         s.left[b] = jnp.concatenate([high, high, low], axis=1)
         score = nt(s.left[b], jnp.concatenate([high, low, high], axis=1))
-        d_score = pair_terms(score, s.cpos[b, :, :nodes], s.cneg[b, :, :nodes])
+        d_score, total = pair_terms(score, s.cpos[b, :, :nodes], s.cneg[b, :, :nodes])
+        s.sm[12:13, 0:1] += total
         s.dz[b] = nn(d_score, high) + tn(d_score, high)
 
     def pair_halo(b):
@@ -353,10 +359,11 @@
         rows = s.zrecv[b].reshape(halo, LANES)[:, :head].astype(BF16)
         high, low = split(nn(rows, whb) + bias[1:2, :])
         score = nt(s.left[b], jnp.concatenate([high, low, high], axis=1))
-        d_score = pair_terms(score, s.cpos[b, :, nodes:], s.cneg[b, :, nodes:])
+        d_score, total = pair_terms(score, s.cpos[b, :, nodes:], s.cneg[b, :, nodes:])
         s.ysend[b, :, :, :head] = tn(d_score, s.left[b, :, :head]).reshape(nd, halo // nd, head)
         scatter_out(s.ysend.at[b], s.yrecv.at[b], 5 + b)
         s.dz[b] += nn(d_score, high)
+        s.sm[12:13, 0:1] += total
 
     def add_to(ref, value, b):
         if b == 0:
@@ -367,7 +374,7 @@
     def back_two(b):
         receive(5 + b)
         returned = s.yrecv[b].reshape(halo, LANES)[:, :head].astype(BF16)
-        dz = s.dz[b] + tn(s.ohs[b], returned)
+        dz = s.dz[b] + nn(s.ohst[b], returned)
         s.sm[11:12, :head] += jnp.sum(dz, axis=0, keepdims=True)
         dz_low = dz.astype(BF16)
         d_out = nt(whb, dz_low)
@@ -584,10 +591,13 @@
     s.gb[...] = jnp.zeros_like(s.gb)
     s.sm[13:14, 0:1] = 2.0 * jnp.sum(plive[...].astype(F32), axis=1, keepdims=True)
     receive(0)
-    stages = [(stage, b) for stage in (layer_one, layer_two, pair_own) for b in range(mb)]
+    slope_one, slope_two = functools.partial(slopes, 0), functools.partial(slopes, 1)
+    stages = [(stage, b) for stage in (layer_one, project_two) for b in range(mb)]
+    stages += [(slope_one, 0)]
+    stages += [(stage, b) for stage in (layer_two, pair_own) for b in range(mb)]
     for b in range(mb):
-        stages += [(pair_halo, b), (functools.partial(slopes, 1), b)]
-    stages += [(functools.partial(slopes, 0), 0)]
+        stages += [(pair_halo, b), (slope_two, b)]
+    stages += [(slope_one, b) for b in range(1, mb)]
     stages += [(back_two, b) for b in range(mb)]
     for stage, b in stages:
         stage(b)
@@ -596,8 +606,6 @@
         after_two(b)
     if split_sum:
         sum_rep(0)
-    for b in range(1, mb):
-        slopes(0, b)
     vector_sum(4)
     s.sm[10:11, :head] = jnp.sum(s.accb[...].T, axis=0, keepdims=True)
     for b in range(mb):
@@ -699,6 +707,7 @@
             chunks[f"agl{chunk}"] = pltpu.VMEM((nd * nr, size, LANES), BF16)
     scratch = dict(
         ohs=pltpu.VMEM((mb, halo, nodes), BF16),
+        ohst=pltpu.VMEM((mb, nodes, halo), BF16),
         fext=pltpu.VMEM((mb, ext, width), BF16),
         fsend=pltpu.VMEM((nd, mb * per, LANES), BF16),
         frecv=pltpu.VMEM((nd, mb * per, LANES), BF16),

time: 55.3 us -> 55.3 us (level)
  no operation moved by 1% of the time
where the time goes in v5:
time: 55.3 us; the launch traced here: 55.1 us
  Pallas kernels  54.2 us (98%)
  between operations  0.83 us (2%)
    pallas_call x1, Pallas kernels, body(): pl.pallas_call(functools.partial(step_kernel, dims, tuple(scratch)), out_...  52.4 us
    pallas_call x1, Pallas kernels, body(): pl.pallas_call(write_kernel, out_shape=scalars + results, in_specs=[whole...  1.8 us

profile of v5, /device:TPU:0, one launch (start us, length us, event | category | flops | bytes accessed | tf_op | source)
XLA Modules:
  0.0 55.1 jit_solution(7774447594752470318)
XLA Ops:
  0.7 52.4 %shard_map.341 = (f32[16,128]{1,0:T(8,128)S(1)}, f32[128,768]{1,0:T(8,128)S(1)}, f32[128,768]{1,0:T(8,128)S(1)}, f32[128,768]{1,0:T(8,128)S(1)}, f32[576,256]{1,...) custom-call(f32[2,256,128]{2,1,0:T(8,128)} %bitcast.20, ...), custom_call_target="tpu_custom_call" | custom-call | tf_op jit(solution)/shard_map/pallas_call | solution.py:782
  53.1 1.8 %shard_map.342 = (f32[1,1]{1,0:T(1,128)}, f32[1,1]{1,0:T(1,128)}, f32[128,768]{1,0:T(8,128)}, f32[128,768]{1,0:T(8,128)}, f32[128,768]{1,0:T(8,128)}, /*index=5*...) custom-call(f32[16,128]{1,0:T(8,128)S(1)} %get-tuple-element.50.refs, ...), custom_call_target="tpu_custom_call" | custom-call | tf_op jit(solution)/shard_map/pallas_call | solution.py:792

commit v6 on v5

--- a/solution.py
+++ b/solution.py
@@ -452,7 +452,7 @@
         return functools.reduce(jnp.add, [ref[i].astype(F32) for i in range(count)])
 
     chunks = len(bounds) - 1
-    split_sum = chunks == 3
+    split_sum = chunks == 4
     in_one, in_two = 3 * hid, 2 * hid + head
     halves = [slice(i * LANES, (i + 1) * LANES) for i in range(hid // LANES)]
     regions, start = [], 0
@@ -571,7 +571,7 @@
             update(4, total[10 + j : 11 + j, :head] * scale, slice(j, j + 1), slice(None))
 
     def chunk_update(chunk):
-        staged_sum = split_sum and chunk < 2
+        staged_sum = split_sum and chunk < 3
         ag = chunk_of(chunk)[4] if staged_sum else direct(chunk)[2]
         receive(4 * chunk + (14 if staged_sum else 12))
         low, high = bounds[chunk], bounds[chunk + 1]
@@ -606,6 +606,7 @@
         after_two(b)
     if split_sum:
         sum_rep(0)
+        sum_rep(1)
     vector_sum(4)
     s.sm[10:11, :head] = jnp.sum(s.accb[...].T, axis=0, keepdims=True)
     for b in range(mb):
@@ -614,27 +615,30 @@
         norm_back(b)
         resid_one(b)
         if final:
-            sum_rep(1)
+            sum_rep(2)
+            sum_dom(1)
         attend_back(0, b)
         weights_one(b)
         if split_sum and b == mb - 2:
             sum_dom(0)
     sum_all(chunks - 1)
     if split_sum:
-        sum_dom(1)
+        sum_dom(2)
         share_dom(0)
+        share_dom(1)
     for j in range(4):
         vector_sum(j)
     small_rep()
     loaded(*range(12, 22))
     if split_sum:
-        share_dom(1)
+        share_dom(2)
     share_all(chunks - 1)
     small_dom()
     if split_sum:
         share_rep(0)
+        share_rep(1)
     if split_sum:
-        share_rep(1)
+        share_rep(2)
     small_update()
     for chunk in range(chunks):
         chunk_update(chunk)
@@ -688,12 +692,12 @@
     rows_all = -(-used // unit) * unit
     bounds = (0, rows_all)
     if quarter % unit == 0 and 2 * hid % unit == 0:
-        bounds = (0, 2 * quarter, rows_all - 2 * hid, rows_all)
+        bounds = (0, quarter, 2 * quarter, rows_all - 2 * hid, rows_all)
     dims = (nd, nr, mb, nodes, fan, hid, head, ext, halo, pairs, bounds)
     chunks = {}
     for chunk in range(len(bounds) - 1):
         rows = bounds[chunk + 1] - bounds[chunk]
-        if len(bounds) > 2 and chunk < 2:
+        if len(bounds) > 2 and chunk < 3:
             size = rows // nr
             chunks[f"rb{chunk}"] = pltpu.VMEM((nr, size, LANES), BF16)
             chunks[f"gd{chunk}"] = pltpu.VMEM((size, LANES), BF16)

time: 55.3 us -> 55.3 us (level)
  no operation moved by 1% of the time
where the time goes in v6:
time: 55.3 us; the launch traced here: 55.1 us
  Pallas kernels  54.3 us (98%)
  between operations  0.83 us (2%)
    pallas_call x1, Pallas kernels, body(): pl.pallas_call(functools.partial(step_kernel, dims, tuple(scratch)), out_...  52.5 us
    pallas_call x1, Pallas kernels, body(): pl.pallas_call(write_kernel, out_shape=scalars + results, in_specs=[whole...  1.8 us

profile of v6, /device:TPU:0, one launch (start us, length us, event | category | flops | bytes accessed | tf_op | source)
XLA Modules:
  0.0 55.1 jit_solution(9780856925521094278)
XLA Ops:
  0.7 52.5 %shard_map.341 = (f32[16,128]{1,0:T(8,128)S(1)}, f32[128,768]{1,0:T(8,128)S(1)}, f32[128,768]{1,0:T(8,128)S(1)}, f32[128,768]{1,0:T(8,128)S(1)}, f32[576,256]{1,...) custom-call(f32[2,256,128]{2,1,0:T(8,128)} %bitcast.20, ...), custom_call_target="tpu_custom_call" | custom-call | tf_op jit(solution)/shard_map/pallas_call | solution.py:786
  53.2 1.8 %shard_map.342 = (f32[1,1]{1,0:T(1,128)}, f32[1,1]{1,0:T(1,128)}, f32[128,768]{1,0:T(8,128)}, f32[128,768]{1,0:T(8,128)}, f32[128,768]{1,0:T(8,128)}, /*index=5*...) custom-call(f32[16,128]{1,0:T(8,128)S(1)} %get-tuple-element.50.refs, ...), custom_call_target="tpu_custom_call" | custom-call | tf_op jit(solution)/shard_map/pallas_call | solution.py:796
